TPU v7x, 768 devices: a whole 4x8x12 slice. The times are simulated.
768 devices in a mesh: ri: 32 (over x, y), ao: 24 (over z, core).
Axes of the slice: x: 4, y: 8, z: 12, core: 2. Of those that a mesh axis runs over, the one named last changes fastest.
Arguments:
- three_centre: bfloat16 [768, 1152, 768], P('ri', 'ao'), may hold values from -6 to 6
- x_mask: int32 [32, 144, 32], P('ri', 'ao'), may hold values 0 or 1
- occ_green: bfloat16 [768, 768], P('ao'), may hold values from -0.21875 to 0.21875
- virt_green: bfloat16 [768, 768], P('ao'), may hold values from -0.21875 to 0.21875
- green_mask: int32 [2, 32, 32], replicated, may hold values 0 or 1
- nu_blocks: int32 [32], replicated, may hold values from 0 to 31, each once
Outputs:
- contracted: bfloat16 [1152, 768, 768], P('ao', 'ri')
Inputs may be any that keep to these rules, and one draw needn't show every extreme that they name: `nu_blocks`: a permutation of the 32 AO blocks.
All inputs are finite; a program needn't handle non-finite values. No bound on the sum of `x_mask` on one device may be relied on, other than what follows from the above.
Results may differ from a plain program's by a relative error of at most 0.0049.
Values may be sent and summed in bfloat16 or wider, within the bound.
No kernel may reach another device: no remote copies, remote signals or barrier semaphores. Data moves between devices by JAX's collectives and lax.ppermute only.
A program may use at most 64 MiB of HBM per device.

v0:
```python
import jax
import jax.numpy as jnp
from jax import lax
from jax.sharding import PartitionSpec as P


def block_mask(row_offset, row_count, block_table, block_size):
    row_blocks = (row_offset + lax.iota(jnp.int32, row_count)) // block_size
    block_count = block_table.shape[0]
    one_hot = (row_blocks[:, None] == lax.iota(jnp.int32, block_count)[None, :]).astype(jnp.float32)
    picked = jnp.dot(one_hot, block_table.astype(jnp.float32))
    widened = jnp.broadcast_to(picked[:, :, None], (row_count, block_count, block_size))
    return widened.reshape(row_count, block_count * block_size).astype(jnp.bfloat16)


def shards(three_centre, x_mask, occ_green, virt_green, green_mask, nu_blocks):
    nu_local, slab_rows, width = three_centre.shape
    block_count = green_mask.shape[1]
    block_size = width // block_count
    local_blocks = x_mask.shape[0]
    ri_blocks = x_mask.shape[1]
    shaped = three_centre.reshape(
        local_blocks, block_size, ri_blocks, slab_rows // ri_blocks, block_count, block_size
    )
    masked_tensor = (shaped * x_mask.astype(jnp.bfloat16)[:, None, :, None, :, None]).reshape(
        nu_local * slab_rows, width
    )
    panel_rows = occ_green.shape[0]
    panel_first = lax.axis_index("ao") * panel_rows
    occ_panel = occ_green * block_mask(panel_first, panel_rows, green_mask[0], block_size)
    virt_panel = virt_green * block_mask(panel_first, panel_rows, green_mask[1], block_size)
    groups = lax.axis_size("ri")
    local_cols = width // groups
    occ_full = lax.all_gather(occ_panel, "ao", axis=0, tiled=True)
    half_done = jnp.dot(masked_tensor, occ_full, preferred_element_type=jnp.float32)
    outgoing = half_done.astype(jnp.bfloat16).reshape(nu_local, slab_rows, groups, local_cols)
    outgoing = outgoing.transpose(0, 2, 1, 3).reshape(nu_local, groups, slab_rows * local_cols)
    regrouped = lax.all_to_all(outgoing, "ri", split_axis=1, concat_axis=0, tiled=True).reshape(
        width, slab_rows * local_cols
    )
    virt_full = lax.all_gather(virt_panel, "ao", axis=0, tiled=True)
    virt_rows = virt_full.reshape(block_count, block_size, width)[nu_blocks].reshape(width, width)
    summed = lax.dot_general(
        regrouped, virt_rows, (((0,), (0,)), ((), ())), preferred_element_type=jnp.float32
    )
    return summed.astype(jnp.bfloat16).reshape(slab_rows, local_cols, width)


def solution(mesh):
    return jax.shard_map(
        shards,
        mesh=mesh,
        in_specs=(P("ri", "ao", None), P("ri", "ao", None), P("ao", None), P("ao", None), P(), P()),
        out_specs=P("ao", "ri", None),
        check_vma=False,
    )
```

profile of v0, /device:TPU:1, one launch (start us, length us, event | category | flops | bytes accessed | tf_op | source)
XLA Modules:
  0.0 192.5 jit_solution(8727542714845394566)
XLA Ops:
  6.6 0.9 convolution_convert_fusion.3
  7.5 0.2 broadcast_in_dim.6
  7.7 0.3 convert_element_type.41
  8.0 1.4 mul.29
  9.4 0.0 all-gather.3.cloned.1.call-update
  9.4 0.7 convert_element_type.37
  10.1 5.9 %mul.25 = bf16[24,6,8,32,24]{4,3,2,1,0:T(8,128)(2,1)} broadcast(bf16[6,32]{1,0:T(8,128)(2,1)S(1)} %bitcast.36), dimensions={1,3} | broadcast | bytes 1769856 | tf_op jit(solution)/shard_map/mul | solution.py:25
  16.1 13.7 %mul.26 = bf16[1152,768]{1,0:T(8,128)(2,1)S(1)} reshape(bf16[24,6,8,32,24]{4,3,2,1,0:T(8,128)(2,1)} %mul.25) | data formatting | bytes 3538944 | tf_op jit(solution)/shard_map/mul | solution.py:25
  29.8 1.5 bitcast_multiply_fusion
  31.3 46.0 %all-gather.3.cloned.1.call-done = bf16[768,768]{1,0:T(8,128)(2,1)} async-done(((bf16[32,768]{1,0:T(8,128)(2,1)}), bf16[768,768]{1,0:T(8,128)(2,1)}) %all-gather.3.cloned.1.call-update) | async-done | bytes 1179664 | tf_op jit(solution)/shard_map/all_gather | solution.py:34
  77.3 3.3 %convolution_convert_fusion.1 = bf16[1152,768]{1,0:T(8,128)(2,1)S(1)} fusion(bf16[1152,768]{1,0:T(8,128)(2,1)} %bitcast_multiply_fusion, bf16[768,768]{1,0:T(8,128)(2,1)} %all-gather.3.cloned.1.call-done), kind=kOutput, calls=%fused_computation.2 | convolution fusion | flops 1359839232 | bytes 4718592 | tf_op jit(solution)/shard_map/dot_general | solution.py:35
  80.6 1.0 copy.10
  81.7 5.6 %reshape.52 = bf16[24,48,32,24]{1,0,3,2:T(8,128)(2,1)} reshape(bf16[1152,768]{0,1:T(8,128)(2,1)S(1)} %copy.10) | data formatting | bytes 3538944 | tf_op jit(solution)/shard_map/reshape | solution.py:36
  87.3 10.6 %copy.13 = bf16[24,32,48,24]{3,2,0,1:T(8,128)(2,1)} copy(bf16[24,32,48,24]{2,0,3,1:T(8,128)(2,1)} %bitcast.32) | data formatting | bytes 3538944 | tf_op jit(solution)/shard_map/reshape | solution.py:37
  97.9 13.4 %reshape.67 = bf16[24,32,1152]{2,0,1:T(8,128)(2,1)} reshape(bf16[24,32,48,24]{3,2,0,1:T(8,128)(2,1)} %copy.13) | data formatting | bytes 3538944 | tf_op jit(solution)/shard_map/reshape | solution.py:37
  111.3 9.4 %all-to-all-start = ((bf16[24,32,1152]{2,0,1:T(8,128)(2,1)}), bf16[24,32,1152]{2,0,1:T(8,128)(2,1)S(1)}, u32[]{:S(2)}, u32[]{:S(2)}) async-start(bf16[24,32,1152]{2,0,1:T(8,128)(2,1)} %reshape.67), calls=%async_computation | async-start | bytes 3538944 | tf_op jit(solution)/shard_map/all_to_all | solution.py:38
  120.7 0.0 all-gather.5.cloned.1.call-start
  120.8 0.2 convolution_convert_fusion.2
  121.0 0.2 broadcast_in_dim.7
  121.2 0.3 convert_element_type.46
  121.5 0.6 mul.30
  122.2 58.7 %all-gather.5.cloned.1.call-done = bf16[768,768]{1,0:T(8,128)(2,1)} async-done(((bf16[32,768]{1,0:T(8,128)(2,1)}), bf16[768,768]{1,0:T(8,128)(2,1)}) %all-gather.5.cloned.1.call-update) | async-done | bytes 1179664 | tf_op jit(solution)/shard_map/all_gather | solution.py:41
  180.9 1.9 gather_fusion
  182.8 2.8 %convolution_convert_fusion = bf16[1152,768]{1,0:T(8,128)(2,1)} fusion(bf16[768,1152]{1,0:T(8,128)(2,1)S(1)} %bitcast.33, bf16[768,768]{1,0:T(8,128)(2,1)S(1)} %bitcast.35), kind=kOutput, calls=%fused_computation.1 | convolution fusion | flops 1359839232 | bytes 4718592 | tf_op jit(solution)/shard_map/dot_general | solution.py:43
  (15 shorter events, 0.1 us)
Async XLA Ops:
  6.5 70.7 %all-gather.3.cloned.1.call-start = ((), (), s32[]{:S(2)}) async-start(), calls=%async_computation.1 | async-start | bytes 1228800 | tf_op jit(solution)/shard_map/all_gather | solution.py:34
  16.1 13.7 %copy-start = (bf16[24,48,768]{2,1,0:T(8,128)(2,1)S(1)}, bf16[24,48,768]{2,1,0:T(8,128)(2,1)}, u32[]{:S(2)}) copy-start(bf16[24,48,768]{2,1,0:T(8,128)(2,1)} %param.6) | copy-start | bytes 5308420
  111.3 9.5 %copy-start.2 = (s32[2,32,32]{2,1,0:T(8,128)S(1)}, s32[2,32,32]{2,1,0:T(8,128)}, u32[]{:S(2)}) copy-start(s32[2,32,32]{2,1,0:T(8,128)} %param.10) | copy-start | bytes 24580
  111.3 10.2 %copy-start.1 = (bf16[32,768]{1,0:T(8,128)(2,1)S(1)}, bf16[32,768]{1,0:T(8,128)(2,1)}, u32[]{:S(2)}) copy-start(bf16[32,768]{1,0:T(8,128)(2,1)} %param.9) | copy-start | bytes 147460
  111.3 10.9 %copy-start.3 = (s32[32]{0:T(128)S(1)}, s32[32]{0:T(128)}, u32[]{:S(2)}) copy-start(s32[32]{0:T(128)} %param.11) | copy-start | bytes 388
  111.3 71.5 %all-to-all-start = ((bf16[24,32,1152]{2,0,1:T(8,128)(2,1)}), bf16[24,32,1152]{2,0,1:T(8,128)(2,1)S(1)}, u32[]{:S(2)}, u32[]{:S(2)}) async-start(bf16[24,32,1152]{2,0,1:T(8,128)(2,1)} %reshape.67), calls=%async_computation | async-start | bytes 3538944 | tf_op jit(solution)/shard_map/all_to_all | solution.py:38
  120.7 60.2 %all-gather.5.cloned.1.call-start = ((), (), s32[]{:S(2)}) async-start(), calls=%async_computation.2 | async-start | bytes 1228800 | tf_op jit(solution)/shard_map/all_gather | solution.py:41
Sparse Core Ops, SparseCore 0:
  9.8 67.4 all-gather.2
  124.0 56.8 all-gather.4
where the time goes:
time: 194 us; the launch traced here: 192 us
  waiting for transfers between devices  105 us (54%)
  local copies, waits for them, and re-layouts  53.2 us (27%)
  between operations  13.5 us (7%)
  starting transfers between devices  9.45 us (5%)
  matrix products  7.23 us (4%)
  other arithmetic  4.28 us (2%)
    all_gather x1, waiting for transfers between devices, shards(): virt_full = lax.all_gather(virt_panel, 'ao', axis=0, tiled=True)  58.7 us
    all_gather x1, waiting for transfers between devices, shards(): occ_full = lax.all_gather(occ_panel, 'ao', axis=0, tiled=True)  46 us
    reshape x2, local copies, waits for them, and re-layouts, shards(): outgoing.transpose(0, 2, 1, 3)  24 us
    mul x2, local copies, waits for them, and re-layouts, shards(): shaped * x_mask.astype(jnp.bfloat16)[:, None, :, None, :, None]  19.6 us
    all_to_all x1, starting transfers between devices, shards(): lax.all_to_all(outgoing, 'ri', split_axis=1, concat_axis=0, tiled=True)  9.4 us
    reshape x1, local copies, waits for them, and re-layouts, shards(): half_done.astype(jnp.bfloat16)  5.64 us
  transfers between devices with their start and end apart: 3, of which 2 were waited for; matrix products, arithmetic and copies ran while one was open for 13% of the time, Pallas kernels for 0%

commit v1 on v0

v1 whole, which is shorter than its diff:
```python
import functools

import jax
import jax.numpy as jnp
from jax import lax
from jax.experimental import pallas as pl
from jax.experimental.pallas import tpu as pltpu
from jax.sharding import PartitionSpec as P

LANES = 128
SUB = 8
GROUP = LANES // SUB
PANEL = 32


def exchange(parts):
    shape = parts[0].shape
    lane_group = lax.broadcasted_iota(jnp.int32, shape, 1) // SUB
    now = [pltpu.roll(part, SUB * p, 1) if p else part for p, part in enumerate(parts)]
    now = [now[(-k) % GROUP] for k in range(GROUP)]
    for bit in (1, 2, 4, 8):
        taken = (lane_group & bit) != 0
        now = [jnp.where(taken, now[(k - bit) % GROUP], now[k]) for k in range(GROUP)]
    return now


def half_kernel(core_ref, x_ref, kept_ref, own_ref, other_ref, out_ref, occ_ref, half_ref):
    rows, slab, width = x_ref.shape

    @pl.when(pl.program_id(0) == 0)
    def _():
        core = core_ref[0]
        for panel in range(own_ref.shape[0] // PANEL):
            here = pl.ds(panel * PANEL, PANEL)
            for ref, place in ((own_ref, core), (other_ref, 1 - core)):
                first = pl.multiple_of((2 * panel + place) * PANEL, PANEL)
                occ_ref[pl.ds(first, PANEL), :] = ref[here, :]

    local_cols = width // out_ref.shape[0]
    kept = kept_ref[0].astype(jnp.float32).astype(jnp.bfloat16)
    block_count = kept.shape[1]
    block = lax.broadcasted_iota(jnp.int32, (block_count, width), 0)
    column = lax.broadcasted_iota(jnp.int32, (block_count, width), 1)
    first = block * (width // block_count)
    spread = ((column >= first) & (column < first + width // block_count)).astype(jnp.float32).astype(jnp.bfloat16)
    wide = jnp.dot(kept, spread, preferred_element_type=jnp.float32)
    ri_rows = slab // kept.shape[0]
    wide = jnp.concatenate(
        [jnp.broadcast_to(wide[i : i + 1], (ri_rows, width)) for i in range(kept.shape[0])], 0
    ).astype(jnp.bfloat16)
    masked = (x_ref[...] * wide[None]).reshape(rows * slab, width)
    highs = out_ref.shape[0] // GROUP
    for third in range(local_cols // SUB):
        columns = pl.ds(third * highs * LANES, highs * LANES)
        half = jnp.dot(masked, occ_ref[:, columns], preferred_element_type=jnp.float32)
        for high in range(highs):
            half_ref[third * highs + high] = half[:, high * LANES : (high + 1) * LANES]
    for third in range(local_cols // SUB):
        for high in range(highs):
            plane = half_ref.at[third * highs + high]
            parts = [plane[pl.ds(p, rows, stride=slab), :] for p in range(slab)]
            for low, part in enumerate(exchange(parts)):
                out_ref[high * GROUP + low, :, pl.ds(third * LANES, LANES)] = part.astype(jnp.bfloat16)


def last_kernel(turn_ref, sent_ref, virt_ref, out_ref, sum_ref):
    slab, local_cols, width = out_ref.shape
    sum_ref[...] = lax.dot_general(
        sent_ref[...], virt_ref[...], (((0,), (0,)), ((), ())), preferred_element_type=jnp.float32
    )
    turn = turn_ref[0]
    for p in range(slab):
        place = lax.rem(p + turn, GROUP)
        pieces = [
            sum_ref[pl.ds(pl.multiple_of(third * LANES + place * SUB, SUB), SUB), :]
            for third in range(local_cols // SUB)
        ]
        out_ref[p] = jnp.concatenate(pieces, 0).astype(jnp.bfloat16)


def half_contract(core, three_centre, x_mask, own, other, groups):
    rows, slab, width = three_centre.shape
    chunks = slab // GROUP
    lanes = width // groups * GROUP
    kept = x_mask.reshape(chunks, -1, x_mask.shape[-1])
    return pl.pallas_call(
        half_kernel,
        grid=(chunks,),
        in_specs=[
            pl.BlockSpec(memory_space=pltpu.SMEM),
            pl.BlockSpec((rows, GROUP, width), lambda c: (0, c, 0)),
            pl.BlockSpec((1,) + kept.shape[1:], lambda c: (c, 0, 0)),
            pl.BlockSpec(own.shape, lambda c: (0, 0)),
            pl.BlockSpec(other.shape, lambda c: (0, 0)),
        ],
        out_specs=pl.BlockSpec((groups, rows, lanes), lambda c: (0, 0, c)),
        out_shape=jax.ShapeDtypeStruct((groups, rows, chunks * lanes), jnp.bfloat16),
        scratch_shapes=[
            pltpu.VMEM((width, width), jnp.bfloat16),
            pltpu.VMEM((width // LANES, rows * GROUP, LANES), jnp.float32),
        ],
        compiler_params=pltpu.CompilerParams(vmem_limit_bytes=60 * 2**20),
        name="half_contract",
    )(core, three_centre, kept, own, other)


def last_contract(sent, virt_rows, turn, slab, local_cols):
    depth, lanes = sent.shape
    width = virt_rows.shape[1]
    chunks = slab // GROUP
    part = lanes // chunks
    return pl.pallas_call(
        last_kernel,
        grid=(chunks,),
        in_specs=[
            pl.BlockSpec(memory_space=pltpu.SMEM),
            pl.BlockSpec((depth, part), lambda c: (0, c)),
            pl.BlockSpec((depth, width), lambda c: (0, 0)),
        ],
        out_specs=pl.BlockSpec((GROUP, local_cols, width), lambda c: (c, 0, 0)),
        out_shape=jax.ShapeDtypeStruct((slab, local_cols, width), jnp.bfloat16),
        scratch_shapes=[pltpu.VMEM((part, width), jnp.float32)],
        compiler_params=pltpu.CompilerParams(vmem_limit_bytes=48 * 2**20),
        name="last_contract",
    )(turn, sent, virt_rows)


def panel_kernel(place_ref, occ_ref, virt_ref, table_ref, occ_out, virt_out):
    rows, width = occ_ref.shape
    count = table_ref.shape[1]
    size = width // count
    row = place_ref[0] * rows + lax.broadcasted_iota(jnp.int32, (rows, count), 0)
    first = lax.broadcasted_iota(jnp.int32, (rows, count), 1) * size
    pick = ((row >= first) & (row < first + size)).astype(jnp.float32)
    column = lax.broadcasted_iota(jnp.int32, (count, width), 1)
    first = lax.broadcasted_iota(jnp.int32, (count, width), 0) * size
    spread = ((column >= first) & (column < first + size)).astype(jnp.float32)

    def masked(ref, table):
        rows_kept = jnp.dot(pick, table.astype(jnp.float32), preferred_element_type=jnp.float32)
        kept = jnp.dot(rows_kept, spread, preferred_element_type=jnp.float32)
        return ref[...] * kept.astype(jnp.bfloat16)

    virt_out[...] = masked(virt_ref, table_ref[1])
    occ = masked(occ_ref, table_ref[0])
    for third in range(size // SUB):
        span = width // (size // SUB)
        source = lax.broadcasted_iota(jnp.int32, (width, span), 0)
        j = lax.broadcasted_iota(jnp.int32, (width, span), 1)
        wanted = (j // SUB) * size + third * SUB + j % SUB
        move = (source == wanted).astype(jnp.float32).astype(jnp.bfloat16)
        part = jnp.dot(occ, move, preferred_element_type=jnp.float32)
        occ_out[:, third * span : (third + 1) * span] = part.astype(jnp.bfloat16)


def panels(place, occ_green, virt_green, green_mask):
    whole = pl.BlockSpec(memory_space=pltpu.VMEM)
    return pl.pallas_call(
        panel_kernel,
        in_specs=[pl.BlockSpec(memory_space=pltpu.SMEM), whole, whole, whole],
        out_specs=[whole, whole],
        out_shape=[
            jax.ShapeDtypeStruct(occ_green.shape, jnp.bfloat16),
            jax.ShapeDtypeStruct(virt_green.shape, jnp.bfloat16),
        ],
        name="panels",
    )(place, occ_green, virt_green, green_mask)


def rows_kernel(core_ref, blocks_ref, own_ref, other_ref, out_ref, full_ref):
    core = core_ref[0]
    for panel in range(own_ref.shape[0] // PANEL):
        here = pl.ds(panel * PANEL, PANEL)
        for ref, place in ((own_ref, core), (other_ref, 1 - core)):
            first = pl.multiple_of((2 * panel + place) * PANEL, PANEL)
            full_ref[pl.ds(first, PANEL), :] = ref[here, :].astype(jnp.float32)
    count, size, _ = out_ref.shape
    for block in range(count):
        first = pl.multiple_of(blocks_ref[block] * size, SUB)
        out_ref[block] = full_ref[pl.ds(first, size), :].astype(jnp.bfloat16)


def block_rows(core, blocks, own, other, size):
    whole = pl.BlockSpec(memory_space=pltpu.VMEM)
    scalars = pl.BlockSpec(memory_space=pltpu.SMEM)
    depth, width = 2 * own.shape[0], own.shape[1]
    return pl.pallas_call(
        rows_kernel,
        in_specs=[scalars, scalars, whole, whole],
        out_specs=whole,
        out_shape=jax.ShapeDtypeStruct((depth // size, size, width), jnp.bfloat16),
        scratch_shapes=[pltpu.VMEM((depth, width), jnp.float32)],
        compiler_params=pltpu.CompilerParams(vmem_limit_bytes=32 * 2**20),
        name="block_rows",
    )(core, blocks, own, other)


def shards(three_centre, x_mask, occ_green, virt_green, green_mask, nu_blocks):
    nu_local, slab, width = three_centre.shape
    block_count = green_mask.shape[1]
    block_size = width // block_count
    groups = lax.axis_size("ri")
    members = lax.axis_size("ao")
    place = lax.axis_index("ao").astype(jnp.int32)
    core = (place % 2)[None]
    same_core = [[z * 2 + c for z in range(members // 2)] for c in range(2)]
    both_cores = [(a, a ^ 1) for a in range(members)]

    def gathered(panel):
        own = lax.all_gather(panel, "ao", axis=0, tiled=True, axis_index_groups=same_core)
        return own, lax.ppermute(own, "ao", both_cores)

    occ_panel, virt_panel = panels(place[None], occ_green, virt_green, green_mask)
    outgoing = half_contract(core, three_centre, x_mask, *gathered(occ_panel), groups)
    outgoing, virt_panel = lax.optimization_barrier((outgoing, virt_panel))
    sent = lax.all_to_all(outgoing, "ri", split_axis=0, concat_axis=0, tiled=True)
    virt_rows = block_rows(core, nu_blocks, *gathered(virt_panel), block_size).reshape(width, width)
    turn = (lax.axis_index("ri") % GROUP).astype(jnp.int32)[None]
    return last_contract(sent.reshape(width, -1), virt_rows, turn, slab, width // groups)


def solution(mesh):
    return jax.shard_map(
        shards,
        mesh=mesh,
        in_specs=(P("ri", "ao", None), P("ri", "ao", None), P("ao", None), P("ao", None), P(), P()),
        out_specs=P("ao", "ri", None),
        check_vma=False,
    )
```

time: 194 us -> 106 us (0.55)
  waiting for transfers between devices: 105 us -> 14.9 us
  blocking collectives: 0 us -> 51.2 us
  local copies, waits for them, and re-layouts: 53.2 us -> 2.7 us
  starting transfers between devices: 9.45 us -> 23.4 us
  between operations: 13.5 us -> 0.08 us
  Pallas kernels: 0 us -> 12 us
  matrix products: 7.23 us -> 0 us
  other arithmetic: 4.28 us -> 0 us
    all_gather x2 -> x0, waiting for transfers between devices: 105 us -> none  [the longest x1 58.7 us: shards(): virt_full = lax.all_gather(virt_panel, 'ao', axis=0, tiled=True)]
    all_gather x0 -> x2, blocking collectives: none -> 51.2 us  [gathered(): lax.all_gather(panel, 'ao', axis=0, tiled=True, axis_index_groups=same_core)]
    reshape x3 -> x0, local copies, waits for them, and re-layouts: 29.6 us -> none  [the longest x2 24 us: shards(): outgoing.transpose(0, 2, 1, 3)]
    mul x2 -> x0, local copies, waits for them, and re-layouts: 19.6 us -> none  [shards(): shaped * x_mask.astype(jnp.bfloat16)[:, None, :, None, :, None]]
    ppermute x0 -> x2, starting transfers between devices: none -> 13.6 us  [gathered(): return (own, lax.ppermute(own, 'ao', both_cores))]
    pallas_call x0 -> x4, Pallas kernels: none -> 12 us  [the longest x1 5.8 us: half_contract(): pl.pallas_call(half_kernel, grid=(chunks,), in_specs=[pl.BlockSpec(memory...]
    all_to_all x1, waiting for transfers between devices: 0.01 us -> 11.7 us  [shards(): lax.all_to_all(outgoing, 'ri', split_axis=0, concat_axis=0, tiled=True)]
    dot_general x4 -> x0, matrix products: 7.23 us -> none  [the longest x1 3.35 us: shards(): jnp.dot(masked_tensor, occ_full, preferred_element_type=jnp.float32)]
  transfers between devices with their start and end apart: 3 -> 3, of which waited for: 2 -> 3; matrix products, arithmetic and copies ran while one was open for 13% -> 0% of each run, Pallas kernels for 0% -> 1%
where the time goes in v1:
time: 106 us; the launch traced here: 104 us
  blocking collectives  51.2 us (48%)
  starting transfers between devices  23.4 us (22%)
  waiting for transfers between devices  14.9 us (14%)
  Pallas kernels  12 us (11%)
  local copies, waits for them, and re-layouts  2.7 us (3%)
    all_gather x2, blocking collectives, gathered(): lax.all_gather(panel, 'ao', axis=0, tiled=True, axis_index_groups=same_core)  51.2 us
    ppermute x2, starting transfers between devices, gathered(): return (own, lax.ppermute(own, 'ao', both_cores))  13.6 us
    all_to_all x1, waiting for transfers between devices, shards(): lax.all_to_all(outgoing, 'ri', split_axis=0, concat_axis=0, tiled=True)  11.7 us
    all_to_all x1, starting transfers between devices, shards(): lax.all_to_all(outgoing, 'ri', split_axis=0, concat_axis=0, tiled=True)  9.82 us
    pallas_call x1, Pallas kernels, half_contract(): pl.pallas_call(half_kernel, grid=(chunks,), in_specs=[pl.BlockSpec(memory...  5.8 us
    pallas_call x1, Pallas kernels, last_contract(): pl.pallas_call(last_kernel, grid=(chunks,), in_specs=[pl.BlockSpec(memory...  3.3 us
    ppermute x2, waiting for transfers between devices, gathered(): return (own, lax.ppermute(own, 'ao', both_cores))  3.18 us
    unnamed x12, local copies, waits for them, and re-layouts  2.7 us
  transfers between devices with their start and end apart: 3, of which 3 were waited for; matrix products, arithmetic and copies ran while one was open for 0% of the time, Pallas kernels for 1%

profile of v1, /device:TPU:1, one launch (start us, length us, event | category | flops | bytes accessed | tf_op | source)
XLA Modules:
  0.0 104.3 jit_solution(11305684277674454797)
XLA Ops:
  0.0 2.1 %panels.1 = (bf16[32,768]{1,0:T(8,128)(2,1)}, bf16[32,768]{1,0:T(8,128)(2,1)}) custom-call(s32[1]{0:T(128)} %bitcast.3.place_ref, bf16[32,768]{1,0:T(8,128)(2,1)} %occ_ref.1, bf16[32,768]{1,0:T(8,128)(2,1)} %virt_ref.1, s32[2,32,32]{2,1,0:T(8,128)} %table_ref.1), custom_call_target="tpu_custom_call" | custom-call | tf_op jit(solution)/shard_map/panels/pallas_call | solution.py:158
  2.1 31.5 %all_gather.6.own_ref = bf16[384,768]{1,0:T(8,128)(2,1)S(1)} all-gather(bf16[32,768]{1,0:T(8,128)(2,1)} %get-tuple-element.9), channel_id=1, replica_groups={{0,2,4,6,8,10,12,14,16,18,20,22},{1,3,5,7,9,11,13,15,17,19,21,23},{24,2..., dimensions={0}, use_global_device_ids=true | all-gather | bytes 638976 | tf_op jit(solution)/shard_map/all_gather | solution.py:210
  33.6 0.0 copy-start.3
  33.6 7.8 %collective-permute-start = (bf16[384,768]{1,0:T(8,128)(2,1)S(1)}, bf16[384,768]{1,0:T(8,128)(2,1)S(1)}, u32[]{:S(2)}, u32[]{:S(2)}) collective-permute-start(bf16[384,768]{1,0:T(8,128)(2,1)S(1)} %all_gather.6.own_ref), channel_id=1, source_target_pairs={{0,1},{1,0},{2,3},{3,2},{4,5},{5,4},{6,7},{7,6},{8,9},{9,8},{10,11... | collective-permute-start | bytes 1769480 | tf_op jit(solution)/shard_map/ppermute | solution.py:211
  41.4 1.6 %collective-permute-done.other_ref = bf16[384,768]{1,0:T(8,128)(2,1)S(1)} collective-permute-done((bf16[384,768]{1,0:T(8,128)(2,1)S(1)}, bf16[384,768]{1,0:T(8,128)(2,1)S(1)}, u32[]{:S(2)}, u32[]{:S(2)}) %collective-permute-start) | collective-permute-done | bytes 589856 | tf_op jit(solution)/shard_map/ppermute | solution.py:211
  43.0 0.0 copy-start.4
  43.0 0.0 copy-done.3
  43.0 0.8 copy-done.4
  43.9 5.8 %half_contract.1 = bf16[32,24,1152]{2,1,0:T(8,128)(2,1)} custom-call(s32[1]{0:T(128)} %bitcast.1.core_ref, bf16[24,48,768]{2,1,0:T(8,128)(2,1)} %x_ref.1, s32[3,2,32]{2,1,0:T(2,128)} %bitcast.8, bf16[384,768]{1,0:T(8,128)(2,1)} %copy-done.3, bf16[384,768]{1,0:T(8,128)(2,1)} %copy-done.4), custom_call_target="tpu_custom_call" | custom-call | tf_op jit(solution)/shard_map/half_contract/pallas_call | solution.py:86
  49.7 0.0 copy-start.5
  49.7 0.0 copy-start.2
  49.7 9.8 %all-to-all-start = ((bf16[32,24,1152]{2,1,0:T(8,128)(2,1)}), bf16[32,24,1152]{2,1,0:T(8,128)(2,1)S(1)}, u32[]{:S(2)}, u32[]{:S(2)}) async-start(bf16[32,24,1152]{2,1,0:T(8,128)(2,1)} %half_contract.1), calls=%async_computation | async-start | bytes 3538944 | tf_op jit(solution)/shard_map/all_to_all | solution.py:216
  59.5 0.0 copy-done.5
  59.5 19.7 %all_gather.7.own_ref = bf16[384,768]{1,0:T(8,128)(2,1)S(1)} all-gather(bf16[32,768]{1,0:T(8,128)(2,1)S(1)} %copy-done.5), channel_id=1, replica_groups={{0,2,4,6,8,10,12,14,16,18,20,22},{1,3,5,7,9,11,13,15,17,19,21,23},{24,2..., dimensions={0}, use_global_device_ids=true | all-gather | bytes 638976 | tf_op jit(solution)/shard_map/all_gather | solution.py:210
  79.2 5.7 %collective-permute-start.1 = (bf16[384,768]{1,0:T(8,128)(2,1)S(1)}, bf16[384,768]{1,0:T(8,128)(2,1)S(1)}, u32[]{:S(2)}, u32[]{:S(2)}) collective-permute-start(bf16[384,768]{1,0:T(8,128)(2,1)S(1)} %all_gather.7.own_ref), channel_id=1, source_target_pairs={{0,1},{1,0},{2,3},{3,2},{4,5},{5,4},{6,7},{7,6},{8,9},{9,8},{10,11... | collective-permute-start | bytes 1769480 | tf_op jit(solution)/shard_map/ppermute | solution.py:211
  85.0 1.6 %collective-permute-done.1.other_ref = bf16[384,768]{1,0:T(8,128)(2,1)S(1)} collective-permute-done((bf16[384,768]{1,0:T(8,128)(2,1)S(1)}, bf16[384,768]{1,0:T(8,128)(2,1)S(1)}, u32[]{:S(2)}, u32[]{:S(2)}) %collective-permute-start.1) | collective-permute-done | bytes 589856 | tf_op jit(solution)/shard_map/ppermute | solution.py:211
  86.6 0.0 copy-start
  86.6 0.8 copy-done
  87.4 0.0 copy-done.2
  87.4 0.0 copy-start.1
  87.4 1.1 %copy-done.1 = bf16[384,768]{1,0:T(8,128)(2,1)S(1)} copy-done((bf16[384,768]{1,0:T(8,128)(2,1)S(1)}, bf16[384,768]{1,0:T(8,128)(2,1)}, u32[]{:S(2)}) %copy-start.1) | copy-done | bytes 589848
  88.5 0.8 block_rows.1
  89.3 11.7 %all-to-all-done = bf16[32,24,1152]{2,1,0:T(8,128)(2,1)S(1)} async-done(((bf16[32,24,1152]{2,1,0:T(8,128)(2,1)}), bf16[32,24,1152]{2,1,0:T(8,128)(2,1)S(1)}, u32[]{:S(2)}, u32[]{:S(2)}) %all-to-all-start) | async-done | bytes 1769504 | tf_op jit(solution)/shard_map/all_to_all | solution.py:216
  101.0 3.3 %last_contract.1 = bf16[48,24,768]{2,1,0:T(8,128)(2,1)} custom-call(s32[1]{0:T(128)} %bitcast.turn_ref, bf16[768,1152]{1,0:T(8,128)(2,1)S(1)} %bitcast.6, bf16[768,768]{1,0:T(8,128)(2,1)S(1)} %bitcast.7), custom_call_target="tpu_custom_call" | custom-call | tf_op jit(solution)/shard_map/last_contract/pallas_call | solution.py:112
Async XLA Ops:
  33.6 9.4 %copy-start.3 = (bf16[384,768]{1,0:T(8,128)(2,1)}, bf16[384,768]{1,0:T(8,128)(2,1)S(1)}, u32[]{:S(2)}) copy-start(bf16[384,768]{1,0:T(8,128)(2,1)S(1)} %all_gather.6.own_ref) | copy-start | bytes 1769476
  33.6 9.4 %collective-permute-start = (bf16[384,768]{1,0:T(8,128)(2,1)S(1)}, bf16[384,768]{1,0:T(8,128)(2,1)S(1)}, u32[]{:S(2)}, u32[]{:S(2)}) collective-permute-start(bf16[384,768]{1,0:T(8,128)(2,1)S(1)} %all_gather.6.own_ref), channel_id=1, source_target_pairs={{0,1},{1,0},{2,3},{3,2},{4,5},{5,4},{6,7},{7,6},{8,9},{9,8},{10,11... | collective-permute-start | bytes 1769480 | tf_op jit(solution)/shard_map/ppermute | solution.py:211
  43.0 0.8 copy-start.4
  49.7 9.8 %copy-start.5 = (bf16[32,768]{1,0:T(8,128)(2,1)S(1)}, bf16[32,768]{1,0:T(8,128)(2,1)}, u32[]{:S(2)}) copy-start(bf16[32,768]{1,0:T(8,128)(2,1)} %get-tuple-element.12) | copy-start | bytes 147460
  49.7 37.7 %copy-start.2 = (s32[32]{0:T(128)S(1)}, s32[32]{0:T(128)}, u32[]{:S(2)}) copy-start(s32[32]{0:T(128)} %blocks_ref.1) | copy-start | bytes 388
  49.7 51.3 %all-to-all-start = ((bf16[32,24,1152]{2,1,0:T(8,128)(2,1)}), bf16[32,24,1152]{2,1,0:T(8,128)(2,1)S(1)}, u32[]{:S(2)}, u32[]{:S(2)}) async-start(bf16[32,24,1152]{2,1,0:T(8,128)(2,1)} %half_contract.1), calls=%async_computation | async-start | bytes 3538944 | tf_op jit(solution)/shard_map/all_to_all | solution.py:216
  79.2 7.4 %collective-permute-start.1 = (bf16[384,768]{1,0:T(8,128)(2,1)S(1)}, bf16[384,768]{1,0:T(8,128)(2,1)S(1)}, u32[]{:S(2)}, u32[]{:S(2)}) collective-permute-start(bf16[384,768]{1,0:T(8,128)(2,1)S(1)} %all_gather.7.own_ref), channel_id=1, source_target_pairs={{0,1},{1,0},{2,3},{3,2},{4,5},{5,4},{6,7},{7,6},{8,9},{9,8},{10,11... | collective-permute-start | bytes 1769480 | tf_op jit(solution)/shard_map/ppermute | solution.py:211
  86.6 0.8 copy-start
  87.4 1.1 %copy-start.1 = (bf16[384,768]{1,0:T(8,128)(2,1)S(1)}, bf16[384,768]{1,0:T(8,128)(2,1)}, u32[]{:S(2)}) copy-start(bf16[384,768]{1,0:T(8,128)(2,1)} %copy-done) | copy-start | bytes 1769476

commit v2 on v1

v2 whole, which is shorter than its diff:
```python
import functools

import jax
import jax.numpy as jnp
from jax import lax
from jax.experimental import pallas as pl
from jax.experimental.pallas import tpu as pltpu
from jax.sharding import PartitionSpec as P

LANES = 128
SUB = 8
GROUP = LANES // SUB
PANEL = 32


def exchange(parts):
    shape = parts[0].shape
    lane_group = lax.broadcasted_iota(jnp.int32, shape, 1) // SUB
    now = [pltpu.roll(part, SUB * p, 1) if p else part for p, part in enumerate(parts)]
    now = [now[(-k) % GROUP] for k in range(GROUP)]
    for bit in (1, 2, 4, 8):
        taken = (lane_group & bit) != 0
        now = [jnp.where(taken, now[(k - bit) % GROUP], now[k]) for k in range(GROUP)]
    return now


def widened(table, width):
    count = table.shape[1]
    size = width // count
    column = lax.broadcasted_iota(jnp.int32, (count, width), 1)
    first = lax.broadcasted_iota(jnp.int32, (count, width), 0) * size
    spread = ((column >= first) & (column < first + size)).astype(jnp.float32).astype(jnp.bfloat16)
    table = table.astype(jnp.float32).astype(jnp.bfloat16)
    return jnp.dot(table, spread, preferred_element_type=jnp.float32)


def half_kernel(core_ref, table_ref, own_ref, other_ref, x_hbm, out_ref, x_ref, keep_ref, occ_ref, half_ref, sems):
    chunk = pl.program_id(0)
    chunks, rows, slab, width = x_ref.shape
    groups = out_ref.shape[0]
    size = width // groups
    copies = [
        pltpu.make_async_copy(x_hbm.at[:, pl.ds(c * slab, slab), :], x_ref.at[c], sems.at[c])
        for c in range(chunks)
    ]

    def place(even_ref, odd_ref):
        for panel in range(width // PANEL):
            ref = odd_ref if panel % 2 else even_ref
            first = panel // 2 * PANEL
            blocks = [(panel * PANEL + row) // size for row in range(0, PANEL, SUB)]
            kept = jnp.concatenate([jnp.broadcast_to(keep_ref[i : i + 1, :], (SUB, width)) for i in blocks], 0)
            occ_ref[panel * PANEL : (panel + 1) * PANEL, :] = ref[first : first + PANEL, :] * kept.astype(jnp.bfloat16)

    @pl.when(chunk == 0)
    def _():
        for copy in copies:
            copy.start()
        keep_ref[...] = widened(table_ref[...], width)
        pl.when(core_ref[0] == 0)(lambda: place(own_ref, other_ref))
        pl.when(core_ref[0] != 0)(lambda: place(other_ref, own_ref))

    for c, copy in enumerate(copies):
        pl.when(chunk == c)(copy.wait)
    ri_rows = SUB
    ri_blocks = slab // ri_rows
    kept = jnp.concatenate(
        [
            jnp.broadcast_to(keep_ref[pl.ds(groups + chunk * ri_blocks + i, 1), :], (ri_rows, width))
            for i in range(ri_blocks)
        ],
        0,
    )
    masked = (x_ref[chunk] * kept.astype(jnp.bfloat16)[None]).reshape(rows * slab, width)
    span = 2 * LANES
    thirds = size // SUB
    for first in range(0, width, span):
        half = jnp.dot(masked, occ_ref[:, first : first + span], preferred_element_type=jnp.float32)
        for part in range(span // LANES):
            half_ref[first // LANES + part] = half[:, part * LANES : (part + 1) * LANES]
    for plane in range(width // LANES):
        part_ref = half_ref.at[plane]
        parts = [part_ref[pl.ds(p, rows, stride=slab), :] for p in range(slab)]
        for low, part in enumerate(exchange(parts)):
            group, third = divmod(plane * GROUP + low, thirds)
            out_ref[group, :, third * LANES : (third + 1) * LANES] = part.astype(jnp.bfloat16)


def last_kernel(turn_ref, sent_ref, virt_ref, out_ref, sum_ref):
    slab, local_cols, width = out_ref.shape
    part = sum_ref.shape[0]
    sent = sent_ref[:, pl.ds(pl.multiple_of(pl.program_id(0) * part, LANES), part)]
    sum_ref[...] = lax.dot_general(
        sent, virt_ref[...], (((0,), (0,)), ((), ())), preferred_element_type=jnp.float32
    )
    turn = turn_ref[0]
    for p in range(slab):
        pieces = [
            sum_ref[pl.ds(pl.multiple_of(third * LANES + lax.rem(p + turn + third, GROUP) * SUB, SUB), SUB), :]
            for third in range(local_cols // SUB)
        ]
        out_ref[p] = jnp.concatenate(pieces, 0).astype(jnp.bfloat16)


def half_contract(core, three_centre, table, own, other, groups):
    rows, slab, width = three_centre.shape
    chunks = slab // GROUP
    lanes = width // groups * GROUP
    whole = pl.BlockSpec(memory_space=pltpu.VMEM)
    return pl.pallas_call(
        half_kernel,
        grid=(chunks,),
        in_specs=[
            pl.BlockSpec(memory_space=pltpu.SMEM),
            whole,
            whole,
            whole,
            pl.BlockSpec(memory_space=pltpu.HBM),
        ],
        out_specs=pl.BlockSpec((groups, rows, lanes), lambda c: (0, 0, c)),
        out_shape=jax.ShapeDtypeStruct((groups, rows, chunks * lanes), jnp.bfloat16),
        scratch_shapes=[
            pltpu.VMEM((chunks, rows, GROUP, width), jnp.bfloat16),
            pltpu.VMEM((table.shape[0], width), jnp.float32),
            pltpu.VMEM((width, width), jnp.bfloat16),
            pltpu.VMEM((width // LANES, rows * GROUP, LANES), jnp.float32),
            pltpu.SemaphoreType.DMA((chunks,)),
        ],
        compiler_params=pltpu.CompilerParams(vmem_limit_bytes=51 * 2**20),
        name="half_contract",
    )(core, table, own, other, three_centre)


def last_contract(sent, virt_rows, turn, slab, local_cols):
    depth, lanes = sent.shape
    width = virt_rows.shape[1]
    chunks = slab // GROUP
    part = lanes // chunks
    return pl.pallas_call(
        last_kernel,
        grid=(chunks,),
        in_specs=[
            pl.BlockSpec(memory_space=pltpu.SMEM),
            pl.BlockSpec(memory_space=pltpu.VMEM),
            pl.BlockSpec(memory_space=pltpu.VMEM),
        ],
        out_specs=pl.BlockSpec((GROUP, local_cols, width), lambda c: (c, 0, 0)),
        out_shape=jax.ShapeDtypeStruct((slab, local_cols, width), jnp.bfloat16),
        scratch_shapes=[pltpu.VMEM((part, width), jnp.float32)],
        compiler_params=pltpu.CompilerParams(vmem_limit_bytes=48 * 2**20),
        name="last_contract",
    )(turn, sent, virt_rows)


def rows_kernel(core_ref, blocks_ref, table_ref, own_ref, other_ref, out_ref, full_ref, kept_ref):
    kept_ref[...] = widened(table_ref[1], own_ref.shape[1])
    core = core_ref[0]
    for panel in range(own_ref.shape[0] // PANEL):
        here = pl.ds(panel * PANEL, PANEL)
        for ref, place in ((own_ref, core), (other_ref, 1 - core)):
            first = pl.multiple_of((2 * panel + place) * PANEL, PANEL)
            full_ref[pl.ds(first, PANEL), :] = ref[here, :].astype(jnp.float32)
    count, size, _ = out_ref.shape
    for block in range(count):
        first = pl.multiple_of(blocks_ref[block] * size, SUB)
        kept = kept_ref[pl.ds(blocks_ref[block], 1), :]
        out_ref[block] = (full_ref[pl.ds(first, size), :] * kept).astype(jnp.bfloat16)


def block_rows(core, blocks, green_mask, own, other, size):
    whole = pl.BlockSpec(memory_space=pltpu.VMEM)
    scalars = pl.BlockSpec(memory_space=pltpu.SMEM)
    depth, width = 2 * own.shape[0], own.shape[1]
    return pl.pallas_call(
        rows_kernel,
        in_specs=[scalars, scalars, whole, whole, whole],
        out_specs=whole,
        out_shape=jax.ShapeDtypeStruct((depth // size, size, width), jnp.bfloat16),
        scratch_shapes=[
            pltpu.VMEM((depth, width), jnp.float32),
            pltpu.VMEM((green_mask.shape[1], width), jnp.float32),
        ],
        compiler_params=pltpu.CompilerParams(vmem_limit_bytes=32 * 2**20),
        name="block_rows",
    )(core, blocks, green_mask, own, other)


def shards(three_centre, x_mask, occ_green, virt_green, green_mask, nu_blocks):
    nu_local, slab, width = three_centre.shape
    block_count = green_mask.shape[1]
    block_size = width // block_count
    groups = lax.axis_size("ri")
    members = lax.axis_size("ao")
    place = lax.axis_index("ao").astype(jnp.int32)
    core = (place % 2)[None]
    same_core = [[z * 2 + c for z in range(members // 2)] for c in range(2)]
    both_cores = [(a, a ^ 1) for a in range(members)]

    def gather(panel):
        return lax.all_gather(panel, "ao", axis=0, tiled=True, axis_index_groups=same_core)

    def swap(half):
        return lax.ppermute(half, "ao", both_cores)

    own, kept, table = lax.optimization_barrier((gather(occ_green), x_mask, green_mask))
    blank = jnp.zeros((-kept.shape[1] % SUB, block_count), jnp.float32)
    table = jnp.concatenate([table[0].astype(jnp.float32), kept[0].astype(jnp.float32), blank], 0)
    outgoing = half_contract(core, three_centre, table, own, swap(own), groups)
    outgoing, virt_panel = lax.optimization_barrier((outgoing, virt_green))
    sent = lax.all_to_all(outgoing, "ri", split_axis=0, concat_axis=0, tiled=True)
    own = gather(virt_panel)
    virt_rows = block_rows(core, nu_blocks, green_mask, own, swap(own), block_size).reshape(width, width)
    turn = (lax.axis_index("ri") * (width // groups // SUB) % GROUP).astype(jnp.int32)[None]
    return last_contract(sent.reshape(width, -1), virt_rows, turn, slab, width // groups)


def solution(mesh):
    return jax.shard_map(
        shards,
        mesh=mesh,
        in_specs=(P("ri", "ao", None), P("ri", "ao", None), P("ao", None), P("ao", None), P(), P()),
        out_specs=P("ao", "ri", None),
        check_vma=False,
    )
```

time: 106 us -> 102 us (0.962)
  Pallas kernels: 12 us -> 9.03 us
  waiting for transfers between devices: 14.9 us -> 12.5 us
  other arithmetic: 0 us -> 1.48 us
    pallas_call x2 -> x1, Pallas kernels: 2.94 us -> 0.92 us  [block_rows(): pl.pallas_call(rows_kernel, in_specs=[scalars, scalars, whole, whole, who...]
    ppermute x2, waiting for transfers between devices: 3.18 us -> 1.61 us  [swap(): return lax.ppermute(half, 'ao', both_cores)]
    convert_element_type x0 -> x2, other arithmetic: none -> 1.41 us  [the longest x1 0.72 us: shards(): table[0].astype(jnp.float32)]
    unnamed x12 -> x10, local copies, waits for them, and re-layouts: 2.7 us -> 2.65 us
  transfers between devices with their start and end apart: 3 -> 3, of which waited for: 3 -> 2; matrix products, arithmetic and copies ran while one was open for 0% -> 2% of each run, Pallas kernels for 1% -> 1%
where the time goes in v2:
time: 102 us; the launch traced here: 100 us
  blocking collectives  51.2 us (50%)
  starting transfers between devices  23.4 us (23%)
  waiting for transfers between devices  12.5 us (12%)
  Pallas kernels  9.03 us (9%)
  local copies, waits for them, and re-layouts  2.73 us (3%)
  other arithmetic  1.48 us (1%)
    all_gather x2, blocking collectives, gather(): lax.all_gather(panel, 'ao', axis=0, tiled=True, axis_index_groups=same_core)  51.2 us
    ppermute x2, starting transfers between devices, swap(): return lax.ppermute(half, 'ao', both_cores)  13.6 us
    all_to_all x1, waiting for transfers between devices, shards(): lax.all_to_all(outgoing, 'ri', split_axis=0, concat_axis=0, tiled=True)  10.9 us
    all_to_all x1, starting transfers between devices, shards(): lax.all_to_all(outgoing, 'ri', split_axis=0, concat_axis=0, tiled=True)  9.81 us
    pallas_call x1, Pallas kernels, half_contract(): pl.pallas_call(half_kernel, grid=(chunks,), in_specs=[pl.BlockSpec(memory...  5.02 us
    pallas_call x1, Pallas kernels, last_contract(): pl.pallas_call(last_kernel, grid=(chunks,), in_specs=[pl.BlockSpec(memory...  3.09 us
    unnamed x10, local copies, waits for them, and re-layouts  2.65 us
  transfers between devices with their start and end apart: 3, of which 2 were waited for; matrix products, arithmetic and copies ran while one was open for 2% of the time, Pallas kernels for 1%

profile of v2, /device:TPU:1, one launch (start us, length us, event | category | flops | bytes accessed | tf_op | source)
XLA Modules:
  0.0 100.4 jit_solution(6996900545360844745)
XLA Ops:
  0.0 31.5 %all_gather.6.own_ref = bf16[384,768]{1,0:T(8,128)(2,1)S(1)} all-gather(bf16[32,768]{1,0:T(8,128)(2,1)} %param.8), channel_id=1, replica_groups={{0,2,4,6,8,10,12,14,16,18,20,22},{1,3,5,7,9,11,13,15,17,19,21,23},{24,2..., dimensions={0}, use_global_device_ids=true | all-gather | bytes 638976 | tf_op jit(solution)/shard_map/all_gather | solution.py:200
  31.5 7.8 %collective-permute-start = (bf16[384,768]{1,0:T(8,128)(2,1)S(1)}, bf16[384,768]{1,0:T(8,128)(2,1)S(1)}, u32[]{:S(2)}, u32[]{:S(2)}) collective-permute-start(bf16[384,768]{1,0:T(8,128)(2,1)S(1)} %all_gather.6.own_ref), channel_id=1, source_target_pairs={{0,1},{1,0},{2,3},{3,2},{4,5},{5,4},{6,7},{7,6},{8,9},{9,8},{10,11... | collective-permute-start | bytes 1769480 | tf_op jit(solution)/shard_map/ppermute | solution.py:203
  39.3 0.1 pad.2.clone
  39.4 0.7 fusion
  40.1 0.7 convert_bitcast_fusion
  40.8 0.1 maximum_maximum_fusion.table_ref
  40.9 0.0 collective-permute-done.other_ref
  40.9 5.0 %half_contract.1 = bf16[32,24,1152]{2,1,0:T(8,128)(2,1)} custom-call(s32[1]{0:T(128)} %bitcast.1.core_ref, f32[40,32]{1,0:T(8,128)S(1)} %maximum_maximum_fusion.table_ref, bf16[384,768]{1,0:T(8,128)(2,1)S(1)} %all_gather.6.own_ref, bf16[384,768]{1,0:T(8,128)(2,1)S(1)} %collective-permute-done.other_ref, bf16[24,48,768]{2,1,0:T(8,128)(2,1)} %x_hbm.1), custom_call_target="tpu_custom_call" | custom-call | tf_op jit(solution)/shard_map/half_contract/pallas_call | solution.py:110
  45.9 0.0 copy-start.4
  45.9 0.0 copy-start.3
  46.0 9.8 %all-to-all-start = ((bf16[32,24,1152]{2,1,0:T(8,128)(2,1)}), bf16[32,24,1152]{2,1,0:T(8,128)(2,1)S(1)}, u32[]{:S(2)}, u32[]{:S(2)}) async-start(bf16[32,24,1152]{2,1,0:T(8,128)(2,1)} %half_contract.1), calls=%async_computation | async-start | bytes 3538944 | tf_op jit(solution)/shard_map/all_to_all | solution.py:210
  55.8 0.0 copy-done.4
  55.8 19.7 %all_gather.7.own_ref = bf16[384,768]{1,0:T(8,128)(2,1)S(1)} all-gather(bf16[32,768]{1,0:T(8,128)(2,1)S(1)} %copy-done.4), channel_id=1, replica_groups={{0,2,4,6,8,10,12,14,16,18,20,22},{1,3,5,7,9,11,13,15,17,19,21,23},{24,2..., dimensions={0}, use_global_device_ids=true | all-gather | bytes 638976 | tf_op jit(solution)/shard_map/all_gather | solution.py:200
  75.5 5.7 %collective-permute-start.1 = (bf16[384,768]{1,0:T(8,128)(2,1)S(1)}, bf16[384,768]{1,0:T(8,128)(2,1)S(1)}, u32[]{:S(2)}, u32[]{:S(2)}) collective-permute-start(bf16[384,768]{1,0:T(8,128)(2,1)S(1)} %all_gather.7.own_ref), channel_id=1, source_target_pairs={{0,1},{1,0},{2,3},{3,2},{4,5},{5,4},{6,7},{7,6},{8,9},{9,8},{10,11... | collective-permute-start | bytes 1769480 | tf_op jit(solution)/shard_map/ppermute | solution.py:203
  81.3 1.6 %collective-permute-done.1.other_ref = bf16[384,768]{1,0:T(8,128)(2,1)S(1)} collective-permute-done((bf16[384,768]{1,0:T(8,128)(2,1)S(1)}, bf16[384,768]{1,0:T(8,128)(2,1)S(1)}, u32[]{:S(2)}, u32[]{:S(2)}) %collective-permute-start.1) | collective-permute-done | bytes 589856 | tf_op jit(solution)/shard_map/ppermute | solution.py:203
  82.9 0.0 copy-start
  82.9 0.8 copy-done
  83.7 0.0 copy-done.3
  83.7 1.1 %copy-done.1 = bf16[384,768]{1,0:T(8,128)(2,1)S(1)} copy-done((bf16[384,768]{1,0:T(8,128)(2,1)S(1)}, bf16[384,768]{1,0:T(8,128)(2,1)}, u32[]{:S(2)}) %copy-start.1) | copy-done | bytes 589848
  84.8 0.0 copy-start.2
  84.8 0.8 copy-done.2
  85.5 0.9 block_rows.1
  86.4 10.9 %all-to-all-done = bf16[32,24,1152]{2,1,0:T(8,128)(2,1)S(1)} async-done(((bf16[32,24,1152]{2,1,0:T(8,128)(2,1)}), bf16[32,24,1152]{2,1,0:T(8,128)(2,1)S(1)}, u32[]{:S(2)}, u32[]{:S(2)}) %all-to-all-start) | async-done | bytes 1769504 | tf_op jit(solution)/shard_map/all_to_all | solution.py:210
  97.3 3.1 %last_contract.1 = bf16[48,24,768]{2,1,0:T(8,128)(2,1)} custom-call(s32[1]{0:T(128)} %bitcast.turn_ref, bf16[768,1152]{1,0:T(8,128)(2,1)S(1)} %bitcast.8, bf16[768,768]{1,0:T(8,128)(2,1)S(1)} %bitcast.9), custom_call_target="tpu_custom_call" | custom-call | tf_op jit(solution)/shard_map/last_contract/pallas_call | solution.py:139
  (2 shorter events, 0.0 us)
Async XLA Ops:
  31.5 9.4 %collective-permute-start = (bf16[384,768]{1,0:T(8,128)(2,1)S(1)}, bf16[384,768]{1,0:T(8,128)(2,1)S(1)}, u32[]{:S(2)}, u32[]{:S(2)}) collective-permute-start(bf16[384,768]{1,0:T(8,128)(2,1)S(1)} %all_gather.6.own_ref), channel_id=1, source_target_pairs={{0,1},{1,0},{2,3},{3,2},{4,5},{5,4},{6,7},{7,6},{8,9},{9,8},{10,11... | collective-permute-start | bytes 1769480 | tf_op jit(solution)/shard_map/ppermute | solution.py:203
  45.9 9.8 %copy-start.4 = (bf16[32,768]{1,0:T(8,128)(2,1)S(1)}, bf16[32,768]{1,0:T(8,128)(2,1)}, u32[]{:S(2)}) copy-start(bf16[32,768]{1,0:T(8,128)(2,1)} %param.9) | copy-start | bytes 147460
  45.9 37.7 %copy-start.3 = (s32[32]{0:T(128)S(1)}, s32[32]{0:T(128)}, u32[]{:S(2)}) copy-start(s32[32]{0:T(128)} %blocks_ref.1) | copy-start | bytes 388
  46.0 51.3 %all-to-all-start = ((bf16[32,24,1152]{2,1,0:T(8,128)(2,1)}), bf16[32,24,1152]{2,1,0:T(8,128)(2,1)S(1)}, u32[]{:S(2)}, u32[]{:S(2)}) async-start(bf16[32,24,1152]{2,1,0:T(8,128)(2,1)} %half_contract.1), calls=%async_computation | async-start | bytes 3538944 | tf_op jit(solution)/shard_map/all_to_all | solution.py:210
  75.5 7.4 %collective-permute-start.1 = (bf16[384,768]{1,0:T(8,128)(2,1)S(1)}, bf16[384,768]{1,0:T(8,128)(2,1)S(1)}, u32[]{:S(2)}, u32[]{:S(2)}) collective-permute-start(bf16[384,768]{1,0:T(8,128)(2,1)S(1)} %all_gather.7.own_ref), channel_id=1, source_target_pairs={{0,1},{1,0},{2,3},{3,2},{4,5},{5,4},{6,7},{7,6},{8,9},{9,8},{10,11... | collective-permute-start | bytes 1769480 | tf_op jit(solution)/shard_map/ppermute | solution.py:203
  82.9 0.8 copy-start
  83.7 1.1 %copy-start.1 = (bf16[384,768]{1,0:T(8,128)(2,1)S(1)}, bf16[384,768]{1,0:T(8,128)(2,1)}, u32[]{:S(2)}) copy-start(bf16[384,768]{1,0:T(8,128)(2,1)} %copy-done) | copy-start | bytes 1769476
  84.8 0.8 copy-start.2

commit v3 on v2

--- a/solution.py
+++ b/solution.py
@@ -34,10 +34,9 @@
     return jnp.dot(table, spread, preferred_element_type=jnp.float32)
 
 
-def half_kernel(core_ref, table_ref, own_ref, other_ref, x_hbm, out_ref, x_ref, keep_ref, occ_ref, half_ref, sems):
-    chunk = pl.program_id(0)
+def half_kernel(core_ref, table_ref, own_ref, other_ref, x_hbm, out_hbm, x_ref, keep_ref, occ_ref, half_ref, out_ref, sems, out_sems):
     chunks, rows, slab, width = x_ref.shape
-    groups = out_ref.shape[0]
+    groups = out_hbm.shape[0]
     size = width // groups
     copies = [
         pltpu.make_async_copy(x_hbm.at[:, pl.ds(c * slab, slab), :], x_ref.at[c], sems.at[c])
@@ -52,54 +51,88 @@
             kept = jnp.concatenate([jnp.broadcast_to(keep_ref[i : i + 1, :], (SUB, width)) for i in blocks], 0)
             occ_ref[panel * PANEL : (panel + 1) * PANEL, :] = ref[first : first + PANEL, :] * kept.astype(jnp.bfloat16)
 
-    @pl.when(chunk == 0)
-    def _():
-        for copy in copies:
+    for copy in copies:
+        copy.start()
+    keep_ref[...] = widened(table_ref[...], width)
+    pl.when(core_ref[0] == 0)(lambda: place(own_ref, other_ref))
+    pl.when(core_ref[0] != 0)(lambda: place(other_ref, own_ref))
+
+    span = 2 * LANES
+    spans = width // span
+    thirds = size // SUB
+    lanes = thirds * LANES
+
+    def masked(c):
+        blocks = [groups + c * slab // SUB + i for i in range(slab // SUB)]
+        kept = jnp.concatenate([jnp.broadcast_to(keep_ref[i : i + 1, :], (SUB, width)) for i in blocks], 0)
+        return (x_ref[c] * kept.astype(jnp.bfloat16)[None]).reshape(rows * slab, width)
+
+    def multiply(step, tensor):
+        first = step % spans * span
+        half = jnp.dot(tensor, occ_ref[:, first : first + span], preferred_element_type=jnp.float32)
+        for part in range(span // LANES):
+            half_ref[step % 2, part] = half[:, part * LANES : (part + 1) * LANES]
+
+    def regroup(step):
+        for part in range(span // LANES):
+            plane = step % spans * (span // LANES) + part
+            part_ref = half_ref.at[step % 2, part]
+            parts = [part_ref[pl.ds(p, rows, stride=slab), :] for p in range(slab)]
+            for low, piece in enumerate(exchange(parts)):
+                group, third = divmod(plane * GROUP + low, thirds)
+                first = step // spans * lanes + third * LANES
+                out_ref[group, :, first : first + LANES] = piece.astype(jnp.bfloat16)
+
+    out_copies = []
+    for step in range(chunks * spans + 1):
+        if step < chunks * spans:
+            if step % spans == 0:
+                copies[step // spans].wait()
+                tensor = masked(step // spans)
+            multiply(step, tensor)
+        if step:
+            regroup(step - 1)
+        if step and step % spans == 0:
+            these = pl.ds((step // spans - 1) * lanes, lanes)
+            copy = pltpu.make_async_copy(
+                out_ref.at[:, :, these], out_hbm.at[:, :, these], out_sems.at[step // spans - 1]
+            )
             copy.start()
-        keep_ref[...] = widened(table_ref[...], width)
-        pl.when(core_ref[0] == 0)(lambda: place(own_ref, other_ref))
-        pl.when(core_ref[0] != 0)(lambda: place(other_ref, own_ref))
-
-    for c, copy in enumerate(copies):
-        pl.when(chunk == c)(copy.wait)
-    ri_rows = SUB
-    ri_blocks = slab // ri_rows
-    kept = jnp.concatenate(
-        [
-            jnp.broadcast_to(keep_ref[pl.ds(groups + chunk * ri_blocks + i, 1), :], (ri_rows, width))
-            for i in range(ri_blocks)
-        ],
-        0,
-    )
-    masked = (x_ref[chunk] * kept.astype(jnp.bfloat16)[None]).reshape(rows * slab, width)
-    span = 2 * LANES
-    thirds = size // SUB
-    for first in range(0, width, span):
-        half = jnp.dot(masked, occ_ref[:, first : first + span], preferred_element_type=jnp.float32)
-        for part in range(span // LANES):
-            half_ref[first // LANES + part] = half[:, part * LANES : (part + 1) * LANES]
-    for plane in range(width // LANES):
-        part_ref = half_ref.at[plane]
-        parts = [part_ref[pl.ds(p, rows, stride=slab), :] for p in range(slab)]
-        for low, part in enumerate(exchange(parts)):
-            group, third = divmod(plane * GROUP + low, thirds)
-            out_ref[group, :, third * LANES : (third + 1) * LANES] = part.astype(jnp.bfloat16)
-
-
-def last_kernel(turn_ref, sent_ref, virt_ref, out_ref, sum_ref):
-    slab, local_cols, width = out_ref.shape
-    part = sum_ref.shape[0]
-    sent = sent_ref[:, pl.ds(pl.multiple_of(pl.program_id(0) * part, LANES), part)]
-    sum_ref[...] = lax.dot_general(
-        sent, virt_ref[...], (((0,), (0,)), ((), ())), preferred_element_type=jnp.float32
-    )
+            out_copies.append(copy)
+    for copy in out_copies:
+        copy.wait()
+
+
+def last_kernel(turn_ref, sent_ref, virt_ref, out_hbm, sum_ref, done_ref, sems):
+    slab, local_cols, width = out_hbm.shape
+    chunks = slab // GROUP
+    part = sent_ref.shape[1] // chunks
     turn = turn_ref[0]
-    for p in range(slab):
-        pieces = [
-            sum_ref[pl.ds(pl.multiple_of(third * LANES + lax.rem(p + turn + third, GROUP) * SUB, SUB), SUB), :]
-            for third in range(local_cols // SUB)
-        ]
-        out_ref[p] = jnp.concatenate(pieces, 0).astype(jnp.bfloat16)
+
+    def multiply(c):
+        sum_ref[c] = lax.dot_general(
+            sent_ref[:, c * part : (c + 1) * part],
+            virt_ref[...],
+            (((0,), (0,)), ((), ())),
+            preferred_element_type=jnp.float32,
+        )
+
+    copies = []
+    multiply(0)
+    for c in range(chunks):
+        if c + 1 < chunks:
+            multiply(c + 1)
+        for p in range(GROUP):
+            pieces = [
+                sum_ref[c, pl.ds(pl.multiple_of(third * LANES + lax.rem(p + turn + third, GROUP) * SUB, SUB), SUB), :]
+                for third in range(local_cols // SUB)
+            ]
+            done_ref[c * GROUP + p] = jnp.concatenate(pieces, 0).astype(jnp.bfloat16)
+        these = pl.ds(c * GROUP, GROUP)
+        copies.append(pltpu.make_async_copy(done_ref.at[these], out_hbm.at[these], sems.at[c]))
+        copies[-1].start()
+    for copy in copies:
+        copy.wait()
 
 
 def half_contract(core, three_centre, table, own, other, groups):
@@ -109,7 +142,6 @@
     whole = pl.BlockSpec(memory_space=pltpu.VMEM)
     return pl.pallas_call(
         half_kernel,
-        grid=(chunks,),
         in_specs=[
             pl.BlockSpec(memory_space=pltpu.SMEM),
             whole,
@@ -117,13 +149,15 @@
             whole,
             pl.BlockSpec(memory_space=pltpu.HBM),
         ],
-        out_specs=pl.BlockSpec((groups, rows, lanes), lambda c: (0, 0, c)),
+        out_specs=pl.BlockSpec(memory_space=pltpu.HBM),
         out_shape=jax.ShapeDtypeStruct((groups, rows, chunks * lanes), jnp.bfloat16),
         scratch_shapes=[
             pltpu.VMEM((chunks, rows, GROUP, width), jnp.bfloat16),
             pltpu.VMEM((table.shape[0], width), jnp.float32),
             pltpu.VMEM((width, width), jnp.bfloat16),
-            pltpu.VMEM((width // LANES, rows * GROUP, LANES), jnp.float32),
+            pltpu.VMEM((2, 2, rows * GROUP, LANES), jnp.float32),
+            pltpu.VMEM((groups, rows, chunks * lanes), jnp.bfloat16),
+            pltpu.SemaphoreType.DMA((chunks,)),
             pltpu.SemaphoreType.DMA((chunks,)),
         ],
         compiler_params=pltpu.CompilerParams(vmem_limit_bytes=51 * 2**20),
@@ -132,21 +166,20 @@
 
 
 def last_contract(sent, virt_rows, turn, slab, local_cols):
-    depth, lanes = sent.shape
+    lanes = sent.shape[1]
     width = virt_rows.shape[1]
     chunks = slab // GROUP
-    part = lanes // chunks
+    whole = pl.BlockSpec(memory_space=pltpu.VMEM)
     return pl.pallas_call(
         last_kernel,
-        grid=(chunks,),
-        in_specs=[
-            pl.BlockSpec(memory_space=pltpu.SMEM),
-            pl.BlockSpec(memory_space=pltpu.VMEM),
-            pl.BlockSpec(memory_space=pltpu.VMEM),
-        ],
-        out_specs=pl.BlockSpec((GROUP, local_cols, width), lambda c: (c, 0, 0)),
+        in_specs=[pl.BlockSpec(memory_space=pltpu.SMEM), whole, whole],
+        out_specs=pl.BlockSpec(memory_space=pltpu.HBM),
         out_shape=jax.ShapeDtypeStruct((slab, local_cols, width), jnp.bfloat16),
-        scratch_shapes=[pltpu.VMEM((part, width), jnp.float32)],
+        scratch_shapes=[
+            pltpu.VMEM((chunks, lanes // chunks, width), jnp.float32),
+            pltpu.VMEM((slab, local_cols, width), jnp.bfloat16),
+            pltpu.SemaphoreType.DMA((chunks,)),
+        ],
         compiler_params=pltpu.CompilerParams(vmem_limit_bytes=48 * 2**20),
         name="last_contract",
     )(turn, sent, virt_rows)

time: 102 us -> 101 us (level)
  no operation moved by 1% of the time
where the time goes in v3:
time: 101 us; the launch traced here: 99.9 us
  blocking collectives  51.2 us (51%)
  starting transfers between devices  23.4 us (23%)
  waiting for transfers between devices  12.5 us (12%)
  Pallas kernels  8.59 us (9%)
  local copies, waits for them, and re-layouts  2.73 us (3%)
  other arithmetic  1.48 us (1%)
    all_gather x2, blocking collectives, gather(): lax.all_gather(panel, 'ao', axis=0, tiled=True, axis_index_groups=same_core)  51.2 us
    ppermute x2, starting transfers between devices, swap(): return lax.ppermute(half, 'ao', both_cores)  13.6 us
    all_to_all x1, waiting for transfers between devices, shards(): lax.all_to_all(outgoing, 'ri', split_axis=0, concat_axis=0, tiled=True)  10.8 us
    all_to_all x1, starting transfers between devices, shards(): lax.all_to_all(outgoing, 'ri', split_axis=0, concat_axis=0, tiled=True)  9.81 us
    pallas_call x1, Pallas kernels, half_contract(): pl.pallas_call(half_kernel, in_specs=[pl.BlockSpec(memory_space=pltpu.SME...  4.95 us
    pallas_call x1, Pallas kernels, last_contract(): pl.pallas_call(last_kernel, in_specs=[pl.BlockSpec(memory_space=pltpu.SME...  2.73 us
    unnamed x10, local copies, waits for them, and re-layouts  2.65 us
  transfers between devices with their start and end apart: 3, of which 2 were waited for; matrix products, arithmetic and copies ran while one was open for 2% of the time, Pallas kernels for 1%

profile of v3, /device:TPU:1, one launch (start us, length us, event | category | flops | bytes accessed | tf_op | source)
XLA Modules:
  0.0 99.9 jit_solution(6432205572589805182)
XLA Ops:
  0.0 31.5 %all_gather.6.own_ref = bf16[384,768]{1,0:T(8,128)(2,1)S(1)} all-gather(bf16[32,768]{1,0:T(8,128)(2,1)} %param.8), channel_id=1, replica_groups={{0,2,4,6,8,10,12,14,16,18,20,22},{1,3,5,7,9,11,13,15,17,19,21,23},{24,2..., dimensions={0}, use_global_device_ids=true | all-gather | bytes 638976 | tf_op jit(solution)/shard_map/all_gather | solution.py:233
  31.5 7.8 %collective-permute-start = (bf16[384,768]{1,0:T(8,128)(2,1)S(1)}, bf16[384,768]{1,0:T(8,128)(2,1)S(1)}, u32[]{:S(2)}, u32[]{:S(2)}) collective-permute-start(bf16[384,768]{1,0:T(8,128)(2,1)S(1)} %all_gather.6.own_ref), channel_id=1, source_target_pairs={{0,1},{1,0},{2,3},{3,2},{4,5},{5,4},{6,7},{7,6},{8,9},{9,8},{10,11... | collective-permute-start | bytes 1769480 | tf_op jit(solution)/shard_map/ppermute | solution.py:236
  39.3 0.1 pad.2.clone
  39.4 0.7 fusion
  40.1 0.7 convert_bitcast_fusion
  40.8 0.1 maximum_maximum_fusion.table_ref
  40.9 0.0 collective-permute-done.other_ref
  40.9 4.9 %half_contract.1 = bf16[32,24,1152]{2,1,0:T(8,128)(2,1)} custom-call(s32[1]{0:T(128)} %bitcast.1.core_ref, f32[40,32]{1,0:T(8,128)S(1)} %maximum_maximum_fusion.table_ref, bf16[384,768]{1,0:T(8,128)(2,1)S(1)} %all_gather.6.own_ref, bf16[384,768]{1,0:T(8,128)(2,1)S(1)} %collective-permute-done.other_ref, bf16[24,48,768]{2,1,0:T(8,128)(2,1)} %x_hbm.1), custom_call_target="tpu_custom_call" | custom-call | tf_op jit(solution)/shard_map/half_contract/pallas_call | solution.py:143
  45.9 0.0 copy-start.4
  45.9 0.0 copy-start.3
  45.9 9.8 %all-to-all-start = ((bf16[32,24,1152]{2,1,0:T(8,128)(2,1)}), bf16[32,24,1152]{2,1,0:T(8,128)(2,1)S(1)}, u32[]{:S(2)}, u32[]{:S(2)}) async-start(bf16[32,24,1152]{2,1,0:T(8,128)(2,1)} %half_contract.1), calls=%async_computation | async-start | bytes 3538944 | tf_op jit(solution)/shard_map/all_to_all | solution.py:243
  55.7 0.0 copy-done.4
  55.7 19.7 %all_gather.7.own_ref = bf16[384,768]{1,0:T(8,128)(2,1)S(1)} all-gather(bf16[32,768]{1,0:T(8,128)(2,1)S(1)} %copy-done.4), channel_id=1, replica_groups={{0,2,4,6,8,10,12,14,16,18,20,22},{1,3,5,7,9,11,13,15,17,19,21,23},{24,2..., dimensions={0}, use_global_device_ids=true | all-gather | bytes 638976 | tf_op jit(solution)/shard_map/all_gather | solution.py:233
  75.4 5.7 %collective-permute-start.1 = (bf16[384,768]{1,0:T(8,128)(2,1)S(1)}, bf16[384,768]{1,0:T(8,128)(2,1)S(1)}, u32[]{:S(2)}, u32[]{:S(2)}) collective-permute-start(bf16[384,768]{1,0:T(8,128)(2,1)S(1)} %all_gather.7.own_ref), channel_id=1, source_target_pairs={{0,1},{1,0},{2,3},{3,2},{4,5},{5,4},{6,7},{7,6},{8,9},{9,8},{10,11... | collective-permute-start | bytes 1769480 | tf_op jit(solution)/shard_map/ppermute | solution.py:236
  81.2 1.6 %collective-permute-done.1.other_ref = bf16[384,768]{1,0:T(8,128)(2,1)S(1)} collective-permute-done((bf16[384,768]{1,0:T(8,128)(2,1)S(1)}, bf16[384,768]{1,0:T(8,128)(2,1)S(1)}, u32[]{:S(2)}, u32[]{:S(2)}) %collective-permute-start.1) | collective-permute-done | bytes 589856 | tf_op jit(solution)/shard_map/ppermute | solution.py:236
  82.8 0.8 copy-done
  83.6 0.0 copy-done.3
  83.6 0.0 copy-start.1
  83.6 1.1 %copy-done.1 = bf16[384,768]{1,0:T(8,128)(2,1)S(1)} copy-done((bf16[384,768]{1,0:T(8,128)(2,1)S(1)}, bf16[384,768]{1,0:T(8,128)(2,1)}, u32[]{:S(2)}) %copy-start.1) | copy-done | bytes 589848
  84.7 0.0 copy-start.2
  84.7 0.8 copy-done.2
  85.4 0.9 block_rows.1
  86.4 10.8 %all-to-all-done = bf16[32,24,1152]{2,1,0:T(8,128)(2,1)S(1)} async-done(((bf16[32,24,1152]{2,1,0:T(8,128)(2,1)}), bf16[32,24,1152]{2,1,0:T(8,128)(2,1)S(1)}, u32[]{:S(2)}, u32[]{:S(2)}) %all-to-all-start) | async-done | bytes 1769504 | tf_op jit(solution)/shard_map/all_to_all | solution.py:243
  97.2 2.7 %last_contract.1 = bf16[48,24,768]{2,1,0:T(8,128)(2,1)} custom-call(s32[1]{0:T(128)} %bitcast.turn_ref, bf16[768,1152]{1,0:T(8,128)(2,1)S(1)} %bitcast.8, bf16[768,768]{1,0:T(8,128)(2,1)S(1)} %bitcast.9), custom_call_target="tpu_custom_call" | custom-call | tf_op jit(solution)/shard_map/last_contract/pallas_call | solution.py:173
  (2 shorter events, 0.0 us)
Async XLA Ops:
  31.5 9.4 %collective-permute-start = (bf16[384,768]{1,0:T(8,128)(2,1)S(1)}, bf16[384,768]{1,0:T(8,128)(2,1)S(1)}, u32[]{:S(2)}, u32[]{:S(2)}) collective-permute-start(bf16[384,768]{1,0:T(8,128)(2,1)S(1)} %all_gather.6.own_ref), channel_id=1, source_target_pairs={{0,1},{1,0},{2,3},{3,2},{4,5},{5,4},{6,7},{7,6},{8,9},{9,8},{10,11... | collective-permute-start | bytes 1769480 | tf_op jit(solution)/shard_map/ppermute | solution.py:236
  45.9 9.8 %copy-start.4 = (bf16[32,768]{1,0:T(8,128)(2,1)S(1)}, bf16[32,768]{1,0:T(8,128)(2,1)}, u32[]{:S(2)}) copy-start(bf16[32,768]{1,0:T(8,128)(2,1)} %param.9) | copy-start | bytes 147460
  45.9 37.7 %copy-start.3 = (s32[32]{0:T(128)S(1)}, s32[32]{0:T(128)}, u32[]{:S(2)}) copy-start(s32[32]{0:T(128)} %blocks_ref.1) | copy-start | bytes 388
  45.9 51.3 %all-to-all-start = ((bf16[32,24,1152]{2,1,0:T(8,128)(2,1)}), bf16[32,24,1152]{2,1,0:T(8,128)(2,1)S(1)}, u32[]{:S(2)}, u32[]{:S(2)}) async-start(bf16[32,24,1152]{2,1,0:T(8,128)(2,1)} %half_contract.1), calls=%async_computation | async-start | bytes 3538944 | tf_op jit(solution)/shard_map/all_to_all | solution.py:243
  75.4 7.4 %collective-permute-start.1 = (bf16[384,768]{1,0:T(8,128)(2,1)S(1)}, bf16[384,768]{1,0:T(8,128)(2,1)S(1)}, u32[]{:S(2)}, u32[]{:S(2)}) collective-permute-start(bf16[384,768]{1,0:T(8,128)(2,1)S(1)} %all_gather.7.own_ref), channel_id=1, source_target_pairs={{0,1},{1,0},{2,3},{3,2},{4,5},{5,4},{6,7},{7,6},{8,9},{9,8},{10,11... | collective-permute-start | bytes 1769480 | tf_op jit(solution)/shard_map/ppermute | solution.py:236
  82.8 0.8 copy-start
  83.6 1.1 %copy-start.1 = (bf16[384,768]{1,0:T(8,128)(2,1)S(1)}, bf16[384,768]{1,0:T(8,128)(2,1)}, u32[]{:S(2)}) copy-start(bf16[384,768]{1,0:T(8,128)(2,1)} %copy-done) | copy-start | bytes 1769476
  84.7 0.8 copy-start.2

commit v4 on v3

--- a/solution.py
+++ b/solution.py
@@ -11,6 +11,7 @@
 SUB = 8
 GROUP = LANES // SUB
 PANEL = 32
+LEAVE = 8
 
 
 def exchange(parts):
@@ -51,8 +52,7 @@
             kept = jnp.concatenate([jnp.broadcast_to(keep_ref[i : i + 1, :], (SUB, width)) for i in blocks], 0)
             occ_ref[panel * PANEL : (panel + 1) * PANEL, :] = ref[first : first + PANEL, :] * kept.astype(jnp.bfloat16)
 
-    for copy in copies:
-        copy.start()
+    copies[0].start()
     keep_ref[...] = widened(table_ref[...], width)
     pl.when(core_ref[0] == 0)(lambda: place(own_ref, other_ref))
     pl.when(core_ref[0] != 0)(lambda: place(other_ref, own_ref))
@@ -88,15 +88,18 @@
         if step < chunks * spans:
             if step % spans == 0:
                 copies[step // spans].wait()
+                if step == 0:
+                    for copy in copies[1:]:
+                        copy.start()
                 tensor = masked(step // spans)
             multiply(step, tensor)
         if step:
             regroup(step - 1)
-        if step and step % spans == 0:
-            these = pl.ds((step // spans - 1) * lanes, lanes)
-            copy = pltpu.make_async_copy(
-                out_ref.at[:, :, these], out_hbm.at[:, :, these], out_sems.at[step // spans - 1]
-            )
+        if step:
+            chunk, part = divmod(step - 1, spans)
+            ready = [i * span // SUB // thirds for i in (part, part + 1)]
+            these = pl.ds(ready[0], ready[1] - ready[0]), slice(None), pl.ds(chunk * lanes, lanes)
+            copy = pltpu.make_async_copy(out_ref.at[these], out_hbm.at[these], out_sems.at[step - 1])
             copy.start()
             out_copies.append(copy)
     for copy in out_copies:
@@ -128,9 +131,10 @@
                 for third in range(local_cols // SUB)
             ]
             done_ref[c * GROUP + p] = jnp.concatenate(pieces, 0).astype(jnp.bfloat16)
-        these = pl.ds(c * GROUP, GROUP)
-        copies.append(pltpu.make_async_copy(done_ref.at[these], out_hbm.at[these], sems.at[c]))
-        copies[-1].start()
+            if (p + 1) % LEAVE == 0:
+                these = pl.ds(c * GROUP + p + 1 - LEAVE, LEAVE)
+                copies.append(pltpu.make_async_copy(done_ref.at[these], out_hbm.at[these], sems.at[len(copies)]))
+                copies[-1].start()
     for copy in copies:
         copy.wait()
 
@@ -158,7 +162,7 @@
             pltpu.VMEM((2, 2, rows * GROUP, LANES), jnp.float32),
             pltpu.VMEM((groups, rows, chunks * lanes), jnp.bfloat16),
             pltpu.SemaphoreType.DMA((chunks,)),
-            pltpu.SemaphoreType.DMA((chunks,)),
+            pltpu.SemaphoreType.DMA((chunks * width // (2 * LANES),)),
         ],
         compiler_params=pltpu.CompilerParams(vmem_limit_bytes=51 * 2**20),
         name="half_contract",
@@ -178,7 +182,7 @@
         scratch_shapes=[
             pltpu.VMEM((chunks, lanes // chunks, width), jnp.float32),
             pltpu.VMEM((slab, local_cols, width), jnp.bfloat16),
-            pltpu.SemaphoreType.DMA((chunks,)),
+            pltpu.SemaphoreType.DMA((slab // LEAVE,)),
         ],
         compiler_params=pltpu.CompilerParams(vmem_limit_bytes=48 * 2**20),
         name="last_contract",

time: 101 us -> 101 us (level)
  no operation moved by 1% of the time
where the time goes in v4:
time: 101 us; the launch traced here: 100 us
  blocking collectives  51.2 us (51%)
  starting transfers between devices  23.4 us (23%)
  waiting for transfers between devices  12.5 us (12%)
  Pallas kernels  8.71 us (9%)
  local copies, waits for them, and re-layouts  2.73 us (3%)
  other arithmetic  1.48 us (1%)
    all_gather x2, blocking collectives, gather(): lax.all_gather(panel, 'ao', axis=0, tiled=True, axis_index_groups=same_core)  51.2 us
    ppermute x2, starting transfers between devices, swap(): return lax.ppermute(half, 'ao', both_cores)  13.6 us
    all_to_all x1, waiting for transfers between devices, shards(): lax.all_to_all(outgoing, 'ri', split_axis=0, concat_axis=0, tiled=True)  10.9 us
    all_to_all x1, starting transfers between devices, shards(): lax.all_to_all(outgoing, 'ri', split_axis=0, concat_axis=0, tiled=True)  9.81 us
    pallas_call x1, Pallas kernels, half_contract(): pl.pallas_call(half_kernel, in_specs=[pl.BlockSpec(memory_space=pltpu.SME...  5.09 us
    pallas_call x1, Pallas kernels, last_contract(): pl.pallas_call(last_kernel, in_specs=[pl.BlockSpec(memory_space=pltpu.SME...  2.71 us
    unnamed x10, local copies, waits for them, and re-layouts  2.65 us
  transfers between devices with their start and end apart: 3, of which 2 were waited for; matrix products, arithmetic and copies ran while one was open for 2% of the time, Pallas kernels for 1%

profile of v4, /device:TPU:1, one launch (start us, length us, event | category | flops | bytes accessed | tf_op | source)
XLA Modules:
  0.0 100.1 jit_solution(7931769655932928549)
XLA Ops:
  0.0 31.5 %all_gather.6.own_ref = bf16[384,768]{1,0:T(8,128)(2,1)S(1)} all-gather(bf16[32,768]{1,0:T(8,128)(2,1)} %param.8), channel_id=1, replica_groups={{0,2,4,6,8,10,12,14,16,18,20,22},{1,3,5,7,9,11,13,15,17,19,21,23},{24,2..., dimensions={0}, use_global_device_ids=true | all-gather | bytes 638976 | tf_op jit(solution)/shard_map/all_gather | solution.py:237
  31.5 7.8 %collective-permute-start = (bf16[384,768]{1,0:T(8,128)(2,1)S(1)}, bf16[384,768]{1,0:T(8,128)(2,1)S(1)}, u32[]{:S(2)}, u32[]{:S(2)}) collective-permute-start(bf16[384,768]{1,0:T(8,128)(2,1)S(1)} %all_gather.6.own_ref), channel_id=1, source_target_pairs={{0,1},{1,0},{2,3},{3,2},{4,5},{5,4},{6,7},{7,6},{8,9},{9,8},{10,11... | collective-permute-start | bytes 1769480 | tf_op jit(solution)/shard_map/ppermute | solution.py:240
  39.3 0.1 pad.2.clone
  39.4 0.7 fusion
  40.1 0.7 convert_bitcast_fusion
  40.8 0.1 maximum_maximum_fusion.table_ref
  40.9 0.0 collective-permute-done.other_ref
  40.9 5.1 %half_contract.1 = bf16[32,24,1152]{2,1,0:T(8,128)(2,1)} custom-call(s32[1]{0:T(128)} %bitcast.1.core_ref, f32[40,32]{1,0:T(8,128)S(1)} %maximum_maximum_fusion.table_ref, bf16[384,768]{1,0:T(8,128)(2,1)S(1)} %all_gather.6.own_ref, bf16[384,768]{1,0:T(8,128)(2,1)S(1)} %collective-permute-done.other_ref, bf16[24,48,768]{2,1,0:T(8,128)(2,1)} %x_hbm.1), custom_call_target="tpu_custom_call" | custom-call | tf_op jit(solution)/shard_map/half_contract/pallas_call | solution.py:147
  46.0 0.0 copy-start.4
  46.0 0.0 copy-start.3
  46.0 9.8 %all-to-all-start = ((bf16[32,24,1152]{2,1,0:T(8,128)(2,1)}), bf16[32,24,1152]{2,1,0:T(8,128)(2,1)S(1)}, u32[]{:S(2)}, u32[]{:S(2)}) async-start(bf16[32,24,1152]{2,1,0:T(8,128)(2,1)} %half_contract.1), calls=%async_computation | async-start | bytes 3538944 | tf_op jit(solution)/shard_map/all_to_all | solution.py:247
  55.8 0.0 copy-done.4
  55.9 19.7 %all_gather.7.own_ref = bf16[384,768]{1,0:T(8,128)(2,1)S(1)} all-gather(bf16[32,768]{1,0:T(8,128)(2,1)S(1)} %copy-done.4), channel_id=1, replica_groups={{0,2,4,6,8,10,12,14,16,18,20,22},{1,3,5,7,9,11,13,15,17,19,21,23},{24,2..., dimensions={0}, use_global_device_ids=true | all-gather | bytes 638976 | tf_op jit(solution)/shard_map/all_gather | solution.py:237
  75.6 5.7 %collective-permute-start.1 = (bf16[384,768]{1,0:T(8,128)(2,1)S(1)}, bf16[384,768]{1,0:T(8,128)(2,1)S(1)}, u32[]{:S(2)}, u32[]{:S(2)}) collective-permute-start(bf16[384,768]{1,0:T(8,128)(2,1)S(1)} %all_gather.7.own_ref), channel_id=1, source_target_pairs={{0,1},{1,0},{2,3},{3,2},{4,5},{5,4},{6,7},{7,6},{8,9},{9,8},{10,11... | collective-permute-start | bytes 1769480 | tf_op jit(solution)/shard_map/ppermute | solution.py:240
  81.3 1.6 %collective-permute-done.1.other_ref = bf16[384,768]{1,0:T(8,128)(2,1)S(1)} collective-permute-done((bf16[384,768]{1,0:T(8,128)(2,1)S(1)}, bf16[384,768]{1,0:T(8,128)(2,1)S(1)}, u32[]{:S(2)}, u32[]{:S(2)}) %collective-permute-start.1) | collective-permute-done | bytes 589856 | tf_op jit(solution)/shard_map/ppermute | solution.py:240
  82.9 0.0 copy-start
  82.9 0.8 copy-done
  83.8 0.0 copy-done.3
  83.8 0.0 copy-start.1
  83.8 1.1 %copy-done.1 = bf16[384,768]{1,0:T(8,128)(2,1)S(1)} copy-done((bf16[384,768]{1,0:T(8,128)(2,1)S(1)}, bf16[384,768]{1,0:T(8,128)(2,1)}, u32[]{:S(2)}) %copy-start.1) | copy-done | bytes 589848
  84.8 0.8 copy-done.2
  85.6 0.9 block_rows.1
  86.5 10.9 %all-to-all-done = bf16[32,24,1152]{2,1,0:T(8,128)(2,1)S(1)} async-done(((bf16[32,24,1152]{2,1,0:T(8,128)(2,1)}), bf16[32,24,1152]{2,1,0:T(8,128)(2,1)S(1)}, u32[]{:S(2)}, u32[]{:S(2)}) %all-to-all-start) | async-done | bytes 1769504 | tf_op jit(solution)/shard_map/all_to_all | solution.py:247
  97.4 2.7 %last_contract.1 = bf16[48,24,768]{2,1,0:T(8,128)(2,1)} custom-call(s32[1]{0:T(128)} %bitcast.turn_ref, bf16[768,1152]{1,0:T(8,128)(2,1)S(1)} %bitcast.8, bf16[768,768]{1,0:T(8,128)(2,1)S(1)} %bitcast.9), custom_call_target="tpu_custom_call" | custom-call | tf_op jit(solution)/shard_map/last_contract/pallas_call | solution.py:177
  (2 shorter events, 0.0 us)
Async XLA Ops:
  31.5 9.4 %collective-permute-start = (bf16[384,768]{1,0:T(8,128)(2,1)S(1)}, bf16[384,768]{1,0:T(8,128)(2,1)S(1)}, u32[]{:S(2)}, u32[]{:S(2)}) collective-permute-start(bf16[384,768]{1,0:T(8,128)(2,1)S(1)} %all_gather.6.own_ref), channel_id=1, source_target_pairs={{0,1},{1,0},{2,3},{3,2},{4,5},{5,4},{6,7},{7,6},{8,9},{9,8},{10,11... | collective-permute-start | bytes 1769480 | tf_op jit(solution)/shard_map/ppermute | solution.py:240
  46.0 9.8 %copy-start.4 = (bf16[32,768]{1,0:T(8,128)(2,1)S(1)}, bf16[32,768]{1,0:T(8,128)(2,1)}, u32[]{:S(2)}) copy-start(bf16[32,768]{1,0:T(8,128)(2,1)} %param.9) | copy-start | bytes 147460
  46.0 37.7 %copy-start.3 = (s32[32]{0:T(128)S(1)}, s32[32]{0:T(128)}, u32[]{:S(2)}) copy-start(s32[32]{0:T(128)} %blocks_ref.1) | copy-start | bytes 388
  46.0 51.3 %all-to-all-start = ((bf16[32,24,1152]{2,1,0:T(8,128)(2,1)}), bf16[32,24,1152]{2,1,0:T(8,128)(2,1)S(1)}, u32[]{:S(2)}, u32[]{:S(2)}) async-start(bf16[32,24,1152]{2,1,0:T(8,128)(2,1)} %half_contract.1), calls=%async_computation | async-start | bytes 3538944 | tf_op jit(solution)/shard_map/all_to_all | solution.py:247
  75.6 7.4 %collective-permute-start.1 = (bf16[384,768]{1,0:T(8,128)(2,1)S(1)}, bf16[384,768]{1,0:T(8,128)(2,1)S(1)}, u32[]{:S(2)}, u32[]{:S(2)}) collective-permute-start(bf16[384,768]{1,0:T(8,128)(2,1)S(1)} %all_gather.7.own_ref), channel_id=1, source_target_pairs={{0,1},{1,0},{2,3},{3,2},{4,5},{5,4},{6,7},{7,6},{8,9},{9,8},{10,11... | collective-permute-start | bytes 1769480 | tf_op jit(solution)/shard_map/ppermute | solution.py:240
  82.9 0.8 copy-start
  83.8 1.1 %copy-start.1 = (bf16[384,768]{1,0:T(8,128)(2,1)S(1)}, bf16[384,768]{1,0:T(8,128)(2,1)}, u32[]{:S(2)}) copy-start(bf16[384,768]{1,0:T(8,128)(2,1)} %copy-done) | copy-start | bytes 1769476
  84.8 0.8 copy-start.2

commit v5 on v3

--- a/solution.py
+++ b/solution.py
@@ -11,6 +11,7 @@
 SUB = 8
 GROUP = LANES // SUB
 PANEL = 32
+PIECE = 6
 
 
 def exchange(parts):
@@ -34,14 +35,34 @@
     return jnp.dot(table, spread, preferred_element_type=jnp.float32)
 
 
-def half_kernel(core_ref, table_ref, own_ref, other_ref, x_hbm, out_hbm, x_ref, keep_ref, occ_ref, half_ref, out_ref, sems, out_sems):
-    chunks, rows, slab, width = x_ref.shape
+def mask_kernel(core_ref, kept_ref, x_hbm, out_ref, sems):
+    del core_ref
+    rows, slab, width = out_ref.shape
+    chunks, in_chunk, count = kept_ref.shape
+    ri_blocks = chunks * in_chunk
+    pieces = [pl.ds(first, PIECE) for first in range(0, rows, PIECE)]
+    copies = [pltpu.make_async_copy(x_hbm.at[r], out_ref.at[r], sems.at[i]) for i, r in enumerate(pieces)]
+    for copy in copies:
+        copy.start()
+    block = lax.broadcasted_iota(jnp.int32, (slab // ri_blocks, width), 1) // (width // count)
+    kept = []
+    for i in range(ri_blocks):
+        word = jnp.int32(0)
+        for b in range(count):
+            word = word | (kept_ref[i // in_chunk, i % in_chunk, b] << b)
+        kept.append(lax.shift_right_logical(jnp.full(block.shape, word), block) & 1)
+    kept = jnp.concatenate(kept, 0).astype(jnp.float32).astype(jnp.bfloat16)
+    for r, copy in zip(pieces, copies):
+        copy.wait()
+        out_ref[r] = out_ref[r] * kept[None]
+
+
+def half_kernel(core_ref, table_ref, own_ref, other_ref, x_ref, out_hbm, keep_ref, occ_ref, half_ref, out_ref, out_sems):
+    rows, ri_rows, width = x_ref.shape
+    slab = GROUP
+    chunks = ri_rows // slab
     groups = out_hbm.shape[0]
     size = width // groups
-    copies = [
-        pltpu.make_async_copy(x_hbm.at[:, pl.ds(c * slab, slab), :], x_ref.at[c], sems.at[c])
-        for c in range(chunks)
-    ]
 
     def place(even_ref, odd_ref):
         for panel in range(width // PANEL):
@@ -51,8 +72,6 @@
             kept = jnp.concatenate([jnp.broadcast_to(keep_ref[i : i + 1, :], (SUB, width)) for i in blocks], 0)
             occ_ref[panel * PANEL : (panel + 1) * PANEL, :] = ref[first : first + PANEL, :] * kept.astype(jnp.bfloat16)
 
-    for copy in copies:
-        copy.start()
     keep_ref[...] = widened(table_ref[...], width)
     pl.when(core_ref[0] == 0)(lambda: place(own_ref, other_ref))
     pl.when(core_ref[0] != 0)(lambda: place(other_ref, own_ref))
@@ -61,11 +80,6 @@
     spans = width // span
     thirds = size // SUB
     lanes = thirds * LANES
-
-    def masked(c):
-        blocks = [groups + c * slab // SUB + i for i in range(slab // SUB)]
-        kept = jnp.concatenate([jnp.broadcast_to(keep_ref[i : i + 1, :], (SUB, width)) for i in blocks], 0)
-        return (x_ref[c] * kept.astype(jnp.bfloat16)[None]).reshape(rows * slab, width)
 
     def multiply(step, tensor):
         first = step % spans * span
@@ -87,8 +101,8 @@
     for step in range(chunks * spans + 1):
         if step < chunks * spans:
             if step % spans == 0:
-                copies[step // spans].wait()
-                tensor = masked(step // spans)
+                first = step // spans * slab
+                tensor = x_ref[:, first : first + slab, :].reshape(rows * slab, width)
             multiply(step, tensor)
         if step:
             regroup(step - 1)
@@ -135,8 +149,22 @@
         copy.wait()
 
 
-def half_contract(core, three_centre, table, own, other, groups):
-    rows, slab, width = three_centre.shape
+def mask_tensor(core, three_centre, x_mask):
+    rows, slab, _ = three_centre.shape
+    scalars = pl.BlockSpec(memory_space=pltpu.SMEM)
+    return pl.pallas_call(
+        mask_kernel,
+        in_specs=[scalars, scalars, pl.BlockSpec(memory_space=pltpu.HBM)],
+        out_specs=pl.BlockSpec(memory_space=pltpu.VMEM),
+        out_shape=jax.ShapeDtypeStruct(three_centre.shape, jnp.bfloat16),
+        scratch_shapes=[pltpu.SemaphoreType.DMA((rows // PIECE,))],
+        compiler_params=pltpu.CompilerParams(vmem_limit_bytes=51 * 2**20),
+        name="mask_tensor",
+    )(core, x_mask.reshape(slab // GROUP, -1, x_mask.shape[-1]), three_centre)
+
+
+def half_contract(core, masked, table, own, other, groups):
+    rows, slab, width = masked.shape
     chunks = slab // GROUP
     lanes = width // groups * GROUP
     whole = pl.BlockSpec(memory_space=pltpu.VMEM)
@@ -147,22 +175,20 @@
             whole,
             whole,
             whole,
-            pl.BlockSpec(memory_space=pltpu.HBM),
+            whole,
         ],
         out_specs=pl.BlockSpec(memory_space=pltpu.HBM),
         out_shape=jax.ShapeDtypeStruct((groups, rows, chunks * lanes), jnp.bfloat16),
         scratch_shapes=[
-            pltpu.VMEM((chunks, rows, GROUP, width), jnp.bfloat16),
             pltpu.VMEM((table.shape[0], width), jnp.float32),
             pltpu.VMEM((width, width), jnp.bfloat16),
             pltpu.VMEM((2, 2, rows * GROUP, LANES), jnp.float32),
             pltpu.VMEM((groups, rows, chunks * lanes), jnp.bfloat16),
             pltpu.SemaphoreType.DMA((chunks,)),
-            pltpu.SemaphoreType.DMA((chunks,)),
-        ],
-        compiler_params=pltpu.CompilerParams(vmem_limit_bytes=51 * 2**20),
+        ],
+        compiler_params=pltpu.CompilerParams(vmem_limit_bytes=32 * 2**20),
         name="half_contract",
-    )(core, table, own, other, three_centre)
+    )(core, table, own, other, masked)
 
 
 def last_contract(sent, virt_rows, turn, slab, local_cols):
@@ -235,10 +261,10 @@
     def swap(half):
         return lax.ppermute(half, "ao", both_cores)
 
-    own, kept, table = lax.optimization_barrier((gather(occ_green), x_mask, green_mask))
-    blank = jnp.zeros((-kept.shape[1] % SUB, block_count), jnp.float32)
-    table = jnp.concatenate([table[0].astype(jnp.float32), kept[0].astype(jnp.float32), blank], 0)
-    outgoing = half_contract(core, three_centre, table, own, swap(own), groups)
+    own, after, table = lax.optimization_barrier((gather(occ_green), core, green_mask))
+    masked = mask_tensor(after, three_centre, x_mask)
+    table = table[0].astype(jnp.float32)
+    outgoing = half_contract(core, masked, table, own, swap(own), groups)
     outgoing, virt_panel = lax.optimization_barrier((outgoing, virt_green))
     sent = lax.all_to_all(outgoing, "ri", split_axis=0, concat_axis=0, tiled=True)
     own = gather(virt_panel)

time: 101 us -> 101 us (level)
  other arithmetic: 1.48 us -> 0.01 us
  waiting for transfers between devices: 12.5 us -> 13.6 us
    pallas_call x0 -> x1, Pallas kernels: none -> 2.06 us  [mask_tensor(): pl.pallas_call(mask_kernel, in_specs=[scalars, scalars, pl.BlockSpec(memo...]
    convert_element_type x2 -> x1, other arithmetic: 1.41 us -> 0.01 us  [shards(): table = table[0].astype(jnp.float32)]
    pallas_call x1, Pallas kernels: 4.95 us -> 3.62 us  [half_contract(): pl.pallas_call(half_kernel, in_specs=[pl.BlockSpec(memory_space=pltpu.SME...]
    all_to_all x1, waiting for transfers between devices: 10.8 us -> 12 us  [shards(): lax.all_to_all(outgoing, 'ri', split_axis=0, concat_axis=0, tiled=True)]
    unnamed x10 -> x14, local copies, waits for them, and re-layouts: 2.65 us -> 3.33 us
  transfers between devices with their start and end apart: 3 -> 3, of which waited for: 2 -> 2; matrix products, arithmetic and copies ran while one was open for 2% -> 0% of each run, Pallas kernels for 1% -> 3%
where the time goes in v5:
time: 101 us
  blocking collectives  50.9 us (50%)
  starting transfers between devices  23.3 us (23%)
  waiting for transfers between devices  13.6 us (13%)
  Pallas kernels  9.31 us (9%)
  local copies, waits for them, and re-layouts  3.33 us (3%)
    all_gather x2, blocking collectives, gather(): lax.all_gather(panel, 'ao', axis=0, tiled=True, axis_index_groups=same_core)  50.9 us
    ppermute x2, starting transfers between devices, swap(): return lax.ppermute(half, 'ao', both_cores)  13.4 us
    all_to_all x1, waiting for transfers between devices, shards(): lax.all_to_all(outgoing, 'ri', split_axis=0, concat_axis=0, tiled=True)  12 us
    all_to_all x1, starting transfers between devices, shards(): lax.all_to_all(outgoing, 'ri', split_axis=0, concat_axis=0, tiled=True)  9.82 us
    pallas_call x1, Pallas kernels, half_contract(): pl.pallas_call(half_kernel, in_specs=[pl.BlockSpec(memory_space=pltpu.SME...  3.62 us
    unnamed x14, local copies, waits for them, and re-layouts  3.33 us
    pallas_call x1, Pallas kernels, last_contract(): pl.pallas_call(last_kernel, in_specs=[pl.BlockSpec(memory_space=pltpu.SME...  2.72 us
    pallas_call x1, Pallas kernels, mask_tensor(): pl.pallas_call(mask_kernel, in_specs=[scalars, scalars, pl.BlockSpec(memo...  2.06 us
  transfers between devices with their start and end apart: 3, of which 2 were waited for; matrix products, arithmetic and copies ran while one was open for 0% of the time, Pallas kernels for 3%

profile of v5, /device:TPU:1, one launch (start us, length us, event | category | flops | bytes accessed | tf_op | source)
XLA Modules:
  0.0 100.6 jit_solution(13176052318097744373)
XLA Ops:
  0.0 31.5 %all_gather.6.own_ref = bf16[384,768]{1,0:T(8,128)(2,1)S(1)} all-gather(bf16[32,768]{1,0:T(8,128)(2,1)} %param.8), channel_id=1, replica_groups={{0,2,4,6,8,10,12,14,16,18,20,22},{1,3,5,7,9,11,13,15,17,19,21,23},{24,2..., dimensions={0}, use_global_device_ids=true | all-gather | bytes 638976 | tf_op jit(solution)/shard_map/all_gather | solution.py:259
  31.5 7.8 %collective-permute-start = (bf16[384,768]{1,0:T(8,128)(2,1)S(1)}, bf16[384,768]{1,0:T(8,128)(2,1)S(1)}, u32[]{:S(2)}, u32[]{:S(2)}) collective-permute-start(bf16[384,768]{1,0:T(8,128)(2,1)S(1)} %all_gather.6.own_ref), channel_id=1, source_target_pairs={{0,1},{1,0},{2,3},{3,2},{4,5},{5,4},{6,7},{7,6},{8,9},{9,8},{10,11... | collective-permute-start | bytes 1769480 | tf_op jit(solution)/shard_map/ppermute | solution.py:262
  39.3 0.0 copy-start.4
  39.3 0.7 copy-done.4
  40.0 0.0 copy-start.2
  40.0 2.1 %mask_tensor.1.x_ref = bf16[24,48,768]{2,1,0:T(8,128)(2,1)S(1)} custom-call(s32[1]{0:T(128)} %bitcast.1.core_ref, s32[3,2,32]{2,1,0:T(2,128)S(1)} %bitcast.9, bf16[24,48,768]{2,1,0:T(8,128)(2,1)} %x_hbm.1), custom_call_target="tpu_custom_call" | custom-call | tf_op jit(solution)/shard_map/mask_tensor/pallas_call | solution.py:155
  42.1 0.0 copy-done.2
  42.1 0.0 collective-permute-done.other_ref
  42.1 3.6 %half_contract.1 = bf16[32,24,1152]{2,1,0:T(8,128)(2,1)} custom-call(s32[1]{0:T(128)} %bitcast.1.core_ref, f32[32,32]{1,0:T(8,128)S(1)} %convert_bitcast_fusion.table_ref, bf16[384,768]{1,0:T(8,128)(2,1)S(1)} %all_gather.6.own_ref, bf16[384,768]{1,0:T(8,128)(2,1)S(1)} %collective-permute-done.other_ref, bf16[24,48,768]{2,1,0:T(8,128)(2,1)S(1)} %mask_tensor.1.x_ref), custom_call_target="tpu_custom_call" | custom-call | tf_op jit(solution)/shard_map/half_contract/pallas_call | solution.py:171
  45.7 0.0 copy-start.6
  45.7 0.0 copy-start.5
  45.7 9.8 %all-to-all-start = ((bf16[32,24,1152]{2,1,0:T(8,128)(2,1)}), bf16[32,24,1152]{2,1,0:T(8,128)(2,1)S(1)}, u32[]{:S(2)}, u32[]{:S(2)}) async-start(bf16[32,24,1152]{2,1,0:T(8,128)(2,1)} %half_contract.1), calls=%async_computation | async-start | bytes 3538944 | tf_op jit(solution)/shard_map/all_to_all | solution.py:269
  55.6 0.0 copy-done.6
  55.6 19.5 %all_gather.7.own_ref = bf16[384,768]{1,0:T(8,128)(2,1)S(1)} all-gather(bf16[32,768]{1,0:T(8,128)(2,1)S(1)} %copy-done.6), channel_id=1, replica_groups={{0,2,4,6,8,10,12,14,16,18,20,22},{1,3,5,7,9,11,13,15,17,19,21,23},{24,2..., dimensions={0}, use_global_device_ids=true | all-gather | bytes 638976 | tf_op jit(solution)/shard_map/all_gather | solution.py:259
  75.0 5.6 %collective-permute-start.1 = (bf16[384,768]{1,0:T(8,128)(2,1)S(1)}, bf16[384,768]{1,0:T(8,128)(2,1)S(1)}, u32[]{:S(2)}, u32[]{:S(2)}) collective-permute-start(bf16[384,768]{1,0:T(8,128)(2,1)S(1)} %all_gather.7.own_ref), channel_id=1, source_target_pairs={{0,1},{1,0},{2,3},{3,2},{4,5},{5,4},{6,7},{7,6},{8,9},{9,8},{10,11... | collective-permute-start | bytes 1769480 | tf_op jit(solution)/shard_map/ppermute | solution.py:262
  80.7 1.6 %collective-permute-done.1.other_ref = bf16[384,768]{1,0:T(8,128)(2,1)S(1)} collective-permute-done((bf16[384,768]{1,0:T(8,128)(2,1)S(1)}, bf16[384,768]{1,0:T(8,128)(2,1)S(1)}, u32[]{:S(2)}, u32[]{:S(2)}) %collective-permute-start.1) | collective-permute-done | bytes 589856 | tf_op jit(solution)/shard_map/ppermute | solution.py:262
  82.3 0.0 copy-start
  82.3 0.8 copy-done
  83.1 0.0 copy-done.5
  83.1 1.1 %copy-done.1 = bf16[384,768]{1,0:T(8,128)(2,1)S(1)} copy-done((bf16[384,768]{1,0:T(8,128)(2,1)S(1)}, bf16[384,768]{1,0:T(8,128)(2,1)}, u32[]{:S(2)}) %copy-start.1) | copy-done | bytes 589848
  84.2 0.8 copy-done.3
  84.9 0.9 block_rows.1
  85.8 12.0 %all-to-all-done = bf16[32,24,1152]{2,1,0:T(8,128)(2,1)S(1)} async-done(((bf16[32,24,1152]{2,1,0:T(8,128)(2,1)}), bf16[32,24,1152]{2,1,0:T(8,128)(2,1)S(1)}, u32[]{:S(2)}, u32[]{:S(2)}) %all-to-all-start) | async-done | bytes 1769504 | tf_op jit(solution)/shard_map/all_to_all | solution.py:269
  97.8 2.7 %last_contract.1 = bf16[48,24,768]{2,1,0:T(8,128)(2,1)} custom-call(s32[1]{0:T(128)} %bitcast.turn_ref, bf16[768,1152]{1,0:T(8,128)(2,1)S(1)} %bitcast.7, bf16[768,768]{1,0:T(8,128)(2,1)S(1)} %bitcast.8), custom_call_target="tpu_custom_call" | custom-call | tf_op jit(solution)/shard_map/last_contract/pallas_call | solution.py:199
  (3 shorter events, 0.0 us)
Async XLA Ops:
  31.5 10.6 %collective-permute-start = (bf16[384,768]{1,0:T(8,128)(2,1)S(1)}, bf16[384,768]{1,0:T(8,128)(2,1)S(1)}, u32[]{:S(2)}, u32[]{:S(2)}) collective-permute-start(bf16[384,768]{1,0:T(8,128)(2,1)S(1)} %all_gather.6.own_ref), channel_id=1, source_target_pairs={{0,1},{1,0},{2,3},{3,2},{4,5},{5,4},{6,7},{7,6},{8,9},{9,8},{10,11... | collective-permute-start | bytes 1769480 | tf_op jit(solution)/shard_map/ppermute | solution.py:262
  39.3 0.7 copy-start.4
  40.0 2.1 %copy-start.2 = (s32[2,32,32]{2,1,0:T(8,128)S(1)}, s32[2,32,32]{2,1,0:T(8,128)}, u32[]{:S(2)}) copy-start(s32[2,32,32]{2,1,0:T(8,128)} %table_ref.1) | copy-start | bytes 24580
  45.7 9.9 %copy-start.6 = (bf16[32,768]{1,0:T(8,128)(2,1)S(1)}, bf16[32,768]{1,0:T(8,128)(2,1)}, u32[]{:S(2)}) copy-start(bf16[32,768]{1,0:T(8,128)(2,1)} %param.9) | copy-start | bytes 147460
  45.7 37.4 %copy-start.5 = (s32[32]{0:T(128)S(1)}, s32[32]{0:T(128)}, u32[]{:S(2)}) copy-start(s32[32]{0:T(128)} %blocks_ref.1) | copy-start | bytes 388
  45.7 52.1 %all-to-all-start = ((bf16[32,24,1152]{2,1,0:T(8,128)(2,1)}), bf16[32,24,1152]{2,1,0:T(8,128)(2,1)S(1)}, u32[]{:S(2)}, u32[]{:S(2)}) async-start(bf16[32,24,1152]{2,1,0:T(8,128)(2,1)} %half_contract.1), calls=%async_computation | async-start | bytes 3538944 | tf_op jit(solution)/shard_map/all_to_all | solution.py:269
  75.0 7.2 %collective-permute-start.1 = (bf16[384,768]{1,0:T(8,128)(2,1)S(1)}, bf16[384,768]{1,0:T(8,128)(2,1)S(1)}, u32[]{:S(2)}, u32[]{:S(2)}) collective-permute-start(bf16[384,768]{1,0:T(8,128)(2,1)S(1)} %all_gather.7.own_ref), channel_id=1, source_target_pairs={{0,1},{1,0},{2,3},{3,2},{4,5},{5,4},{6,7},{7,6},{8,9},{9,8},{10,11... | collective-permute-start | bytes 1769480 | tf_op jit(solution)/shard_map/ppermute | solution.py:262
  82.3 0.8 copy-start
  83.1 1.1 %copy-start.1 = (bf16[384,768]{1,0:T(8,128)(2,1)S(1)}, bf16[384,768]{1,0:T(8,128)(2,1)}, u32[]{:S(2)}) copy-start(bf16[384,768]{1,0:T(8,128)(2,1)} %copy-done) | copy-start | bytes 1769476
  84.2 0.8 copy-start.3

commit v6 on v3

--- a/solution.py
+++ b/solution.py
@@ -11,6 +11,7 @@
 SUB = 8
 GROUP = LANES // SUB
 PANEL = 32
+PIECE = 6
 
 
 def exchange(parts):
@@ -34,14 +35,22 @@
     return jnp.dot(table, spread, preferred_element_type=jnp.float32)
 
 
-def half_kernel(core_ref, table_ref, own_ref, other_ref, x_hbm, out_hbm, x_ref, keep_ref, occ_ref, half_ref, out_ref, sems, out_sems):
-    chunks, rows, slab, width = x_ref.shape
+def fetch_kernel(core_ref, x_hbm, out_ref, sems):
+    del core_ref
+    pieces = [pl.ds(first, PIECE) for first in range(0, out_ref.shape[0], PIECE)]
+    copies = [pltpu.make_async_copy(x_hbm.at[r], out_ref.at[r], sems.at[i]) for i, r in enumerate(pieces)]
+    for copy in copies:
+        copy.start()
+    for copy in copies:
+        copy.wait()
+
+
+def half_kernel(core_ref, table_ref, own_ref, other_ref, x_ref, out_hbm, keep_ref, occ_ref, half_ref, out_ref, out_sems):
+    rows, ri_rows, width = x_ref.shape
+    slab = GROUP
+    chunks = ri_rows // slab
     groups = out_hbm.shape[0]
     size = width // groups
-    copies = [
-        pltpu.make_async_copy(x_hbm.at[:, pl.ds(c * slab, slab), :], x_ref.at[c], sems.at[c])
-        for c in range(chunks)
-    ]
 
     def place(even_ref, odd_ref):
         for panel in range(width // PANEL):
@@ -51,8 +60,6 @@
             kept = jnp.concatenate([jnp.broadcast_to(keep_ref[i : i + 1, :], (SUB, width)) for i in blocks], 0)
             occ_ref[panel * PANEL : (panel + 1) * PANEL, :] = ref[first : first + PANEL, :] * kept.astype(jnp.bfloat16)
 
-    for copy in copies:
-        copy.start()
     keep_ref[...] = widened(table_ref[...], width)
     pl.when(core_ref[0] == 0)(lambda: place(own_ref, other_ref))
     pl.when(core_ref[0] != 0)(lambda: place(other_ref, own_ref))
@@ -65,7 +72,7 @@
     def masked(c):
         blocks = [groups + c * slab // SUB + i for i in range(slab // SUB)]
         kept = jnp.concatenate([jnp.broadcast_to(keep_ref[i : i + 1, :], (SUB, width)) for i in blocks], 0)
-        return (x_ref[c] * kept.astype(jnp.bfloat16)[None]).reshape(rows * slab, width)
+        return (x_ref[:, c * slab : (c + 1) * slab, :] * kept.astype(jnp.bfloat16)[None]).reshape(rows * slab, width)
 
     def multiply(step, tensor):
         first = step % spans * span
@@ -87,7 +94,6 @@
     for step in range(chunks * spans + 1):
         if step < chunks * spans:
             if step % spans == 0:
-                copies[step // spans].wait()
                 tensor = masked(step // spans)
             multiply(step, tensor)
         if step:
@@ -135,6 +141,18 @@
         copy.wait()
 
 
+def fetch(core, three_centre):
+    return pl.pallas_call(
+        fetch_kernel,
+        in_specs=[pl.BlockSpec(memory_space=pltpu.SMEM), pl.BlockSpec(memory_space=pltpu.HBM)],
+        out_specs=pl.BlockSpec(memory_space=pltpu.VMEM),
+        out_shape=jax.ShapeDtypeStruct(three_centre.shape, jnp.bfloat16),
+        scratch_shapes=[pltpu.SemaphoreType.DMA((three_centre.shape[0] // PIECE,))],
+        compiler_params=pltpu.CompilerParams(vmem_limit_bytes=51 * 2**20),
+        name="fetch",
+    )(core, three_centre)
+
+
 def half_contract(core, three_centre, table, own, other, groups):
     rows, slab, width = three_centre.shape
     chunks = slab // GROUP
@@ -147,20 +165,18 @@
             whole,
             whole,
             whole,
-            pl.BlockSpec(memory_space=pltpu.HBM),
+            whole,
         ],
         out_specs=pl.BlockSpec(memory_space=pltpu.HBM),
         out_shape=jax.ShapeDtypeStruct((groups, rows, chunks * lanes), jnp.bfloat16),
         scratch_shapes=[
-            pltpu.VMEM((chunks, rows, GROUP, width), jnp.bfloat16),
             pltpu.VMEM((table.shape[0], width), jnp.float32),
             pltpu.VMEM((width, width), jnp.bfloat16),
             pltpu.VMEM((2, 2, rows * GROUP, LANES), jnp.float32),
             pltpu.VMEM((groups, rows, chunks * lanes), jnp.bfloat16),
             pltpu.SemaphoreType.DMA((chunks,)),
-            pltpu.SemaphoreType.DMA((chunks,)),
-        ],
-        compiler_params=pltpu.CompilerParams(vmem_limit_bytes=51 * 2**20),
+        ],
+        compiler_params=pltpu.CompilerParams(vmem_limit_bytes=32 * 2**20),
         name="half_contract",
     )(core, table, own, other, three_centre)
 
@@ -235,10 +251,11 @@
     def swap(half):
         return lax.ppermute(half, "ao", both_cores)
 
-    own, kept, table = lax.optimization_barrier((gather(occ_green), x_mask, green_mask))
+    own, after = lax.optimization_barrier((gather(occ_green), core))
+    tensor, kept, table = lax.optimization_barrier((fetch(after, three_centre), x_mask, green_mask))
     blank = jnp.zeros((-kept.shape[1] % SUB, block_count), jnp.float32)
     table = jnp.concatenate([table[0].astype(jnp.float32), kept[0].astype(jnp.float32), blank], 0)
-    outgoing = half_contract(core, three_centre, table, own, swap(own), groups)
+    outgoing = half_contract(core, tensor, table, own, swap(own), groups)
     outgoing, virt_panel = lax.optimization_barrier((outgoing, virt_green))
     sent = lax.all_to_all(outgoing, "ri", split_axis=0, concat_axis=0, tiled=True)
     own = gather(virt_panel)

time: 101 us -> 100 us (0.990)
  other arithmetic: 1.48 us -> 0.08 us
    pallas_call x0 -> x1, Pallas kernels: none -> 1.45 us  [fetch(): pl.pallas_call(fetch_kernel, in_specs=[pl.BlockSpec(memory_space=pltpu.SM...]
    pallas_call x1, Pallas kernels: 4.95 us -> 3.75 us  [half_contract(): pl.pallas_call(half_kernel, in_specs=[pl.BlockSpec(memory_space=pltpu.SME...]
    unnamed x10 -> x14, local copies, waits for them, and re-layouts: 2.65 us -> 2.65 us
  transfers between devices with their start and end apart: 3 -> 3, of which waited for: 2 -> 2; matrix products, arithmetic and copies ran while one was open for 2% -> 0% of each run, Pallas kernels for 1% -> 2%
where the time goes in v6:
time: 100 us; the launch traced here: 98.9 us
  blocking collectives  51.2 us (51%)
  starting transfers between devices  23.5 us (24%)
  waiting for transfers between devices  12.5 us (12%)
  Pallas kernels  8.84 us (9%)
  local copies, waits for them, and re-layouts  2.73 us (3%)
    all_gather x2, blocking collectives, gather(): lax.all_gather(panel, 'ao', axis=0, tiled=True, axis_index_groups=same_core)  51.2 us
    ppermute x2, starting transfers between devices, swap(): return lax.ppermute(half, 'ao', both_cores)  13.7 us
    all_to_all x1, waiting for transfers between devices, shards(): lax.all_to_all(outgoing, 'ri', split_axis=0, concat_axis=0, tiled=True)  10.9 us
    all_to_all x1, starting transfers between devices, shards(): lax.all_to_all(outgoing, 'ri', split_axis=0, concat_axis=0, tiled=True)  9.82 us
    pallas_call x1, Pallas kernels, half_contract(): pl.pallas_call(half_kernel, in_specs=[pl.BlockSpec(memory_space=pltpu.SME...  3.75 us
    pallas_call x1, Pallas kernels, last_contract(): pl.pallas_call(last_kernel, in_specs=[pl.BlockSpec(memory_space=pltpu.SME...  2.73 us
    unnamed x14, local copies, waits for them, and re-layouts  2.65 us
  transfers between devices with their start and end apart: 3, of which 2 were waited for; matrix products, arithmetic and copies ran while one was open for 0% of the time, Pallas kernels for 2%

profile of v6, /device:TPU:1, one launch (start us, length us, event | category | flops | bytes accessed | tf_op | source)
XLA Modules:
  0.0 98.9 jit_solution(12529721353207445561)
XLA Ops:
  0.0 31.5 %all_gather.6.own_ref = bf16[384,768]{1,0:T(8,128)(2,1)S(1)} all-gather(bf16[32,768]{1,0:T(8,128)(2,1)} %param.8), channel_id=1, replica_groups={{0,2,4,6,8,10,12,14,16,18,20,22},{1,3,5,7,9,11,13,15,17,19,21,23},{24,2..., dimensions={0}, use_global_device_ids=true | all-gather | bytes 638976 | tf_op jit(solution)/shard_map/all_gather | solution.py:249
  31.5 0.0 copy-start.6
  31.5 8.0 %collective-permute-start = (bf16[384,768]{1,0:T(8,128)(2,1)S(1)}, bf16[384,768]{1,0:T(8,128)(2,1)S(1)}, u32[]{:S(2)}, u32[]{:S(2)}) collective-permute-start(bf16[384,768]{1,0:T(8,128)(2,1)S(1)} %all_gather.6.own_ref), channel_id=1, source_target_pairs={{0,1},{1,0},{2,3},{3,2},{4,5},{5,4},{6,7},{7,6},{8,9},{9,8},{10,11... | collective-permute-start | bytes 1769480 | tf_op jit(solution)/shard_map/ppermute | solution.py:252
  39.4 1.4 %fetch.1.x_ref = bf16[24,48,768]{2,1,0:T(8,128)(2,1)S(1)} custom-call(s32[1]{0:T(128)} %bitcast.1.core_ref, bf16[24,48,768]{2,1,0:T(8,128)(2,1)} %x_hbm.1), custom_call_target="tpu_custom_call" | custom-call | tf_op jit(solution)/shard_map/fetch/pallas_call | solution.py:145
  40.9 0.1 pad.2.clone
  41.0 0.0 copy-done.6
  41.0 0.0 copy-done.2
  41.0 0.1 maximum_maximum_fusion.table_ref
  41.1 0.0 collective-permute-done.other_ref
  41.1 3.7 %half_contract.1 = bf16[32,24,1152]{2,1,0:T(8,128)(2,1)} custom-call(s32[1]{0:T(128)} %bitcast.1.core_ref, f32[40,32]{1,0:T(8,128)S(1)} %maximum_maximum_fusion.table_ref, bf16[384,768]{1,0:T(8,128)(2,1)S(1)} %all_gather.6.own_ref, bf16[384,768]{1,0:T(8,128)(2,1)S(1)} %collective-permute-done.other_ref, bf16[24,48,768]{2,1,0:T(8,128)(2,1)S(1)} %fetch.1.x_ref), custom_call_target="tpu_custom_call" | custom-call | tf_op jit(solution)/shard_map/half_contract/pallas_call | solution.py:161
  44.8 0.0 copy-start.5
  44.8 0.0 copy-start.4
  44.9 9.8 %all-to-all-start = ((bf16[32,24,1152]{2,1,0:T(8,128)(2,1)}), bf16[32,24,1152]{2,1,0:T(8,128)(2,1)S(1)}, u32[]{:S(2)}, u32[]{:S(2)}) async-start(bf16[32,24,1152]{2,1,0:T(8,128)(2,1)} %half_contract.1), calls=%async_computation | async-start | bytes 3538944 | tf_op jit(solution)/shard_map/all_to_all | solution.py:260
  54.7 0.0 copy-done.5
  54.7 19.7 %all_gather.7.own_ref = bf16[384,768]{1,0:T(8,128)(2,1)S(1)} all-gather(bf16[32,768]{1,0:T(8,128)(2,1)S(1)} %copy-done.5), channel_id=1, replica_groups={{0,2,4,6,8,10,12,14,16,18,20,22},{1,3,5,7,9,11,13,15,17,19,21,23},{24,2..., dimensions={0}, use_global_device_ids=true | all-gather | bytes 638976 | tf_op jit(solution)/shard_map/all_gather | solution.py:249
  74.4 5.7 %collective-permute-start.1 = (bf16[384,768]{1,0:T(8,128)(2,1)S(1)}, bf16[384,768]{1,0:T(8,128)(2,1)S(1)}, u32[]{:S(2)}, u32[]{:S(2)}) collective-permute-start(bf16[384,768]{1,0:T(8,128)(2,1)S(1)} %all_gather.7.own_ref), channel_id=1, source_target_pairs={{0,1},{1,0},{2,3},{3,2},{4,5},{5,4},{6,7},{7,6},{8,9},{9,8},{10,11... | collective-permute-start | bytes 1769480 | tf_op jit(solution)/shard_map/ppermute | solution.py:252
  80.1 1.6 %collective-permute-done.1.other_ref = bf16[384,768]{1,0:T(8,128)(2,1)S(1)} collective-permute-done((bf16[384,768]{1,0:T(8,128)(2,1)S(1)}, bf16[384,768]{1,0:T(8,128)(2,1)S(1)}, u32[]{:S(2)}, u32[]{:S(2)}) %collective-permute-start.1) | collective-permute-done | bytes 589856 | tf_op jit(solution)/shard_map/ppermute | solution.py:252
  81.7 0.8 copy-done
  82.5 0.0 copy-done.4
  82.6 1.1 %copy-done.1 = bf16[384,768]{1,0:T(8,128)(2,1)S(1)} copy-done((bf16[384,768]{1,0:T(8,128)(2,1)S(1)}, bf16[384,768]{1,0:T(8,128)(2,1)}, u32[]{:S(2)}) %copy-start.1) | copy-done | bytes 589848
  83.6 0.8 copy-done.3
  84.4 0.9 block_rows.1
  85.3 10.9 %all-to-all-done = bf16[32,24,1152]{2,1,0:T(8,128)(2,1)S(1)} async-done(((bf16[32,24,1152]{2,1,0:T(8,128)(2,1)}), bf16[32,24,1152]{2,1,0:T(8,128)(2,1)S(1)}, u32[]{:S(2)}, u32[]{:S(2)}) %all-to-all-start) | async-done | bytes 1769504 | tf_op jit(solution)/shard_map/all_to_all | solution.py:260
  96.2 2.7 %last_contract.1 = bf16[48,24,768]{2,1,0:T(8,128)(2,1)} custom-call(s32[1]{0:T(128)} %bitcast.turn_ref, bf16[768,1152]{1,0:T(8,128)(2,1)S(1)} %bitcast.8, bf16[768,768]{1,0:T(8,128)(2,1)S(1)} %bitcast.9), custom_call_target="tpu_custom_call" | custom-call | tf_op jit(solution)/shard_map/last_contract/pallas_call | solution.py:189
  (7 shorter events, 0.0 us)
Async XLA Ops:
  31.5 9.5 %copy-start.6 = (s32[1,6,32]{2,0,1:T(1,128)S(1)}, s32[1,6,32]{2,0,1:T(1,128)}, u32[]{:S(2)}) copy-start(s32[1,6,32]{2,0,1:T(1,128)} %param.7) | copy-start | bytes 2308
  31.5 9.5 %copy-start.2 = (s32[2,32,32]{2,1,0:T(8,128)S(1)}, s32[2,32,32]{2,1,0:T(8,128)}, u32[]{:S(2)}) copy-start(s32[2,32,32]{2,1,0:T(8,128)} %table_ref.1) | copy-start | bytes 24580
  31.5 9.6 %collective-permute-start = (bf16[384,768]{1,0:T(8,128)(2,1)S(1)}, bf16[384,768]{1,0:T(8,128)(2,1)S(1)}, u32[]{:S(2)}, u32[]{:S(2)}) collective-permute-start(bf16[384,768]{1,0:T(8,128)(2,1)S(1)} %all_gather.6.own_ref), channel_id=1, source_target_pairs={{0,1},{1,0},{2,3},{3,2},{4,5},{5,4},{6,7},{7,6},{8,9},{9,8},{10,11... | collective-permute-start | bytes 1769480 | tf_op jit(solution)/shard_map/ppermute | solution.py:252
  44.8 9.9 %copy-start.5 = (bf16[32,768]{1,0:T(8,128)(2,1)S(1)}, bf16[32,768]{1,0:T(8,128)(2,1)}, u32[]{:S(2)}) copy-start(bf16[32,768]{1,0:T(8,128)(2,1)} %param.9) | copy-start | bytes 147460
  44.8 37.7 %copy-start.4 = (s32[32]{0:T(128)S(1)}, s32[32]{0:T(128)}, u32[]{:S(2)}) copy-start(s32[32]{0:T(128)} %blocks_ref.1) | copy-start | bytes 388
  44.9 51.3 %all-to-all-start = ((bf16[32,24,1152]{2,1,0:T(8,128)(2,1)}), bf16[32,24,1152]{2,1,0:T(8,128)(2,1)S(1)}, u32[]{:S(2)}, u32[]{:S(2)}) async-start(bf16[32,24,1152]{2,1,0:T(8,128)(2,1)} %half_contract.1), calls=%async_computation | async-start | bytes 3538944 | tf_op jit(solution)/shard_map/all_to_all | solution.py:260
  74.4 7.3 %collective-permute-start.1 = (bf16[384,768]{1,0:T(8,128)(2,1)S(1)}, bf16[384,768]{1,0:T(8,128)(2,1)S(1)}, u32[]{:S(2)}, u32[]{:S(2)}) collective-permute-start(bf16[384,768]{1,0:T(8,128)(2,1)S(1)} %all_gather.7.own_ref), channel_id=1, source_target_pairs={{0,1},{1,0},{2,3},{3,2},{4,5},{5,4},{6,7},{7,6},{8,9},{9,8},{10,11... | collective-permute-start | bytes 1769480 | tf_op jit(solution)/shard_map/ppermute | solution.py:252
  81.7 0.8 copy-start
  82.5 1.1 %copy-start.1 = (bf16[384,768]{1,0:T(8,128)(2,1)S(1)}, bf16[384,768]{1,0:T(8,128)(2,1)}, u32[]{:S(2)}) copy-start(bf16[384,768]{1,0:T(8,128)(2,1)} %copy-done) | copy-start | bytes 1769476
  83.6 0.8 copy-start.3

commit v7 on v6

--- a/solution.py
+++ b/solution.py
@@ -52,18 +52,19 @@
     groups = out_hbm.shape[0]
     size = width // groups
 
-    def place(even_ref, odd_ref):
+    first_core = core_ref[0] == 0
+
+    def place(columns):
         for panel in range(width // PANEL):
-            ref = odd_ref if panel % 2 else even_ref
-            first = panel // 2 * PANEL
+            here = pl.ds(panel // 2 * PANEL, PANEL)
+            pair = (own_ref[here, columns], other_ref[here, columns])
+            rows_of = lax.select(first_core, pair[panel % 2], pair[1 - panel % 2])
             blocks = [(panel * PANEL + row) // size for row in range(0, PANEL, SUB)]
-            kept = jnp.concatenate([jnp.broadcast_to(keep_ref[i : i + 1, :], (SUB, width)) for i in blocks], 0)
-            occ_ref[panel * PANEL : (panel + 1) * PANEL, :] = ref[first : first + PANEL, :] * kept.astype(jnp.bfloat16)
+            kept = [jnp.broadcast_to(keep_ref[i : i + 1, columns], (SUB, span)) for i in blocks]
+            there = pl.ds(panel * PANEL, PANEL)
+            occ_ref[there, columns] = rows_of * jnp.concatenate(kept, 0).astype(jnp.bfloat16)
 
     keep_ref[...] = widened(table_ref[...], width)
-    pl.when(core_ref[0] == 0)(lambda: place(own_ref, other_ref))
-    pl.when(core_ref[0] != 0)(lambda: place(other_ref, own_ref))
-
     span = 2 * LANES
     spans = width // span
     thirds = size // SUB
@@ -95,6 +96,8 @@
         if step < chunks * spans:
             if step % spans == 0:
                 tensor = masked(step // spans)
+            if step < spans:
+                place(pl.ds(step * span, span))
             multiply(step, tensor)
         if step:
             regroup(step - 1)

time: 100 us -> 99.7 us (level)
  no operation moved by 1% of the time
where the time goes in v7:
time: 99.7 us; the launch traced here: 98.4 us
  blocking collectives  51.2 us (51%)
  starting transfers between devices  23.5 us (24%)
  waiting for transfers between devices  12.5 us (13%)
  Pallas kernels  8.42 us (8%)
  local copies, waits for them, and re-layouts  2.73 us (3%)
    all_gather x2, blocking collectives, gather(): lax.all_gather(panel, 'ao', axis=0, tiled=True, axis_index_groups=same_core)  51.2 us
    ppermute x2, starting transfers between devices, swap(): return lax.ppermute(half, 'ao', both_cores)  13.7 us
    all_to_all x1, waiting for transfers between devices, shards(): lax.all_to_all(outgoing, 'ri', split_axis=0, concat_axis=0, tiled=True)  10.9 us
    all_to_all x1, starting transfers between devices, shards(): lax.all_to_all(outgoing, 'ri', split_axis=0, concat_axis=0, tiled=True)  9.8 us
    pallas_call x1, Pallas kernels, half_contract(): pl.pallas_call(half_kernel, in_specs=[pl.BlockSpec(memory_space=pltpu.SME...  3.33 us
    pallas_call x1, Pallas kernels, last_contract(): pl.pallas_call(last_kernel, in_specs=[pl.BlockSpec(memory_space=pltpu.SME...  2.73 us
    unnamed x14, local copies, waits for them, and re-layouts  2.65 us
  transfers between devices with their start and end apart: 3, of which 2 were waited for; matrix products, arithmetic and copies ran while one was open for 0% of the time, Pallas kernels for 2%

profile of v7, /device:TPU:1, one launch (start us, length us, event | category | flops | bytes accessed | tf_op | source)
XLA Modules:
  0.0 98.4 jit_solution(14854476151540646861)
XLA Ops:
  0.0 31.5 %all_gather.6.own_ref = bf16[384,768]{1,0:T(8,128)(2,1)S(1)} all-gather(bf16[32,768]{1,0:T(8,128)(2,1)} %param.8), channel_id=1, replica_groups={{0,2,4,6,8,10,12,14,16,18,20,22},{1,3,5,7,9,11,13,15,17,19,21,23},{24,2..., dimensions={0}, use_global_device_ids=true | all-gather | bytes 638976 | tf_op jit(solution)/shard_map/all_gather | solution.py:252
  31.5 0.0 copy-start.6
  31.5 8.0 %collective-permute-start = (bf16[384,768]{1,0:T(8,128)(2,1)S(1)}, bf16[384,768]{1,0:T(8,128)(2,1)S(1)}, u32[]{:S(2)}, u32[]{:S(2)}) collective-permute-start(bf16[384,768]{1,0:T(8,128)(2,1)S(1)} %all_gather.6.own_ref), channel_id=1, source_target_pairs={{0,1},{1,0},{2,3},{3,2},{4,5},{5,4},{6,7},{7,6},{8,9},{9,8},{10,11... | collective-permute-start | bytes 1769480 | tf_op jit(solution)/shard_map/ppermute | solution.py:255
  39.4 1.4 %fetch.1.x_ref = bf16[24,48,768]{2,1,0:T(8,128)(2,1)S(1)} custom-call(s32[1]{0:T(128)} %bitcast.1.core_ref, bf16[24,48,768]{2,1,0:T(8,128)(2,1)} %x_hbm.1), custom_call_target="tpu_custom_call" | custom-call | tf_op jit(solution)/shard_map/fetch/pallas_call | solution.py:148
  40.9 0.1 pad.2.clone
  41.0 0.0 copy-done.6
  41.0 0.0 copy-done.2
  41.0 0.1 maximum_maximum_fusion.table_ref
  41.1 0.0 collective-permute-done.other_ref
  41.1 3.3 %half_contract.1 = bf16[32,24,1152]{2,1,0:T(8,128)(2,1)} custom-call(s32[1]{0:T(128)} %bitcast.1.core_ref, f32[40,32]{1,0:T(8,128)S(1)} %maximum_maximum_fusion.table_ref, bf16[384,768]{1,0:T(8,128)(2,1)S(1)} %all_gather.6.own_ref, bf16[384,768]{1,0:T(8,128)(2,1)S(1)} %collective-permute-done.other_ref, bf16[24,48,768]{2,1,0:T(8,128)(2,1)S(1)} %fetch.1.x_ref), custom_call_target="tpu_custom_call" | custom-call | tf_op jit(solution)/shard_map/half_contract/pallas_call | solution.py:164
  44.4 0.0 copy-start.5
  44.4 0.0 copy-start.4
  44.4 9.8 %all-to-all-start = ((bf16[32,24,1152]{2,1,0:T(8,128)(2,1)}), bf16[32,24,1152]{2,1,0:T(8,128)(2,1)S(1)}, u32[]{:S(2)}, u32[]{:S(2)}) async-start(bf16[32,24,1152]{2,1,0:T(8,128)(2,1)} %half_contract.1), calls=%async_computation | async-start | bytes 3538944 | tf_op jit(solution)/shard_map/all_to_all | solution.py:263
  54.2 0.0 copy-done.5
  54.3 19.7 %all_gather.7.own_ref = bf16[384,768]{1,0:T(8,128)(2,1)S(1)} all-gather(bf16[32,768]{1,0:T(8,128)(2,1)S(1)} %copy-done.5), channel_id=1, replica_groups={{0,2,4,6,8,10,12,14,16,18,20,22},{1,3,5,7,9,11,13,15,17,19,21,23},{24,2..., dimensions={0}, use_global_device_ids=true | all-gather | bytes 638976 | tf_op jit(solution)/shard_map/all_gather | solution.py:252
  74.0 5.7 %collective-permute-start.1 = (bf16[384,768]{1,0:T(8,128)(2,1)S(1)}, bf16[384,768]{1,0:T(8,128)(2,1)S(1)}, u32[]{:S(2)}, u32[]{:S(2)}) collective-permute-start(bf16[384,768]{1,0:T(8,128)(2,1)S(1)} %all_gather.7.own_ref), channel_id=1, source_target_pairs={{0,1},{1,0},{2,3},{3,2},{4,5},{5,4},{6,7},{7,6},{8,9},{9,8},{10,11... | collective-permute-start | bytes 1769480 | tf_op jit(solution)/shard_map/ppermute | solution.py:255
  79.7 1.6 %collective-permute-done.1.other_ref = bf16[384,768]{1,0:T(8,128)(2,1)S(1)} collective-permute-done((bf16[384,768]{1,0:T(8,128)(2,1)S(1)}, bf16[384,768]{1,0:T(8,128)(2,1)S(1)}, u32[]{:S(2)}, u32[]{:S(2)}) %collective-permute-start.1) | collective-permute-done | bytes 589856 | tf_op jit(solution)/shard_map/ppermute | solution.py:255
  81.3 0.8 copy-done
  82.1 0.0 copy-done.4
  82.1 1.1 %copy-done.1 = bf16[384,768]{1,0:T(8,128)(2,1)S(1)} copy-done((bf16[384,768]{1,0:T(8,128)(2,1)S(1)}, bf16[384,768]{1,0:T(8,128)(2,1)}, u32[]{:S(2)}) %copy-start.1) | copy-done | bytes 589848
  83.2 0.8 copy-done.3
  83.9 0.9 block_rows.1
  84.9 10.9 %all-to-all-done = bf16[32,24,1152]{2,1,0:T(8,128)(2,1)S(1)} async-done(((bf16[32,24,1152]{2,1,0:T(8,128)(2,1)}), bf16[32,24,1152]{2,1,0:T(8,128)(2,1)S(1)}, u32[]{:S(2)}, u32[]{:S(2)}) %all-to-all-start) | async-done | bytes 1769504 | tf_op jit(solution)/shard_map/all_to_all | solution.py:263
  95.7 2.7 %last_contract.1 = bf16[48,24,768]{2,1,0:T(8,128)(2,1)} custom-call(s32[1]{0:T(128)} %bitcast.turn_ref, bf16[768,1152]{1,0:T(8,128)(2,1)S(1)} %bitcast.8, bf16[768,768]{1,0:T(8,128)(2,1)S(1)} %bitcast.9), custom_call_target="tpu_custom_call" | custom-call | tf_op jit(solution)/shard_map/last_contract/pallas_call | solution.py:192
  (7 shorter events, 0.0 us)
Async XLA Ops:
  31.5 9.5 %copy-start.6 = (s32[1,6,32]{2,0,1:T(1,128)S(1)}, s32[1,6,32]{2,0,1:T(1,128)}, u32[]{:S(2)}) copy-start(s32[1,6,32]{2,0,1:T(1,128)} %param.7) | copy-start | bytes 2308
  31.5 9.5 %copy-start.2 = (s32[2,32,32]{2,1,0:T(8,128)S(1)}, s32[2,32,32]{2,1,0:T(8,128)}, u32[]{:S(2)}) copy-start(s32[2,32,32]{2,1,0:T(8,128)} %table_ref.1) | copy-start | bytes 24580
  31.5 9.6 %collective-permute-start = (bf16[384,768]{1,0:T(8,128)(2,1)S(1)}, bf16[384,768]{1,0:T(8,128)(2,1)S(1)}, u32[]{:S(2)}, u32[]{:S(2)}) collective-permute-start(bf16[384,768]{1,0:T(8,128)(2,1)S(1)} %all_gather.6.own_ref), channel_id=1, source_target_pairs={{0,1},{1,0},{2,3},{3,2},{4,5},{5,4},{6,7},{7,6},{8,9},{9,8},{10,11... | collective-permute-start | bytes 1769480 | tf_op jit(solution)/shard_map/ppermute | solution.py:255
  44.4 9.8 %copy-start.5 = (bf16[32,768]{1,0:T(8,128)(2,1)S(1)}, bf16[32,768]{1,0:T(8,128)(2,1)}, u32[]{:S(2)}) copy-start(bf16[32,768]{1,0:T(8,128)(2,1)} %param.9) | copy-start | bytes 147460
  44.4 37.7 %copy-start.4 = (s32[32]{0:T(128)S(1)}, s32[32]{0:T(128)}, u32[]{:S(2)}) copy-start(s32[32]{0:T(128)} %blocks_ref.1) | copy-start | bytes 388
  44.4 51.3 %all-to-all-start = ((bf16[32,24,1152]{2,1,0:T(8,128)(2,1)}), bf16[32,24,1152]{2,1,0:T(8,128)(2,1)S(1)}, u32[]{:S(2)}, u32[]{:S(2)}) async-start(bf16[32,24,1152]{2,1,0:T(8,128)(2,1)} %half_contract.1), calls=%async_computation | async-start | bytes 3538944 | tf_op jit(solution)/shard_map/all_to_all | solution.py:263
  74.0 7.3 %collective-permute-start.1 = (bf16[384,768]{1,0:T(8,128)(2,1)S(1)}, bf16[384,768]{1,0:T(8,128)(2,1)S(1)}, u32[]{:S(2)}, u32[]{:S(2)}) collective-permute-start(bf16[384,768]{1,0:T(8,128)(2,1)S(1)} %all_gather.7.own_ref), channel_id=1, source_target_pairs={{0,1},{1,0},{2,3},{3,2},{4,5},{5,4},{6,7},{7,6},{8,9},{9,8},{10,11... | collective-permute-start | bytes 1769480 | tf_op jit(solution)/shard_map/ppermute | solution.py:255
  81.3 0.8 copy-start
  82.1 1.1 %copy-start.1 = (bf16[384,768]{1,0:T(8,128)(2,1)S(1)}, bf16[384,768]{1,0:T(8,128)(2,1)}, u32[]{:S(2)}) copy-start(bf16[384,768]{1,0:T(8,128)(2,1)} %copy-done) | copy-start | bytes 1769476
  83.2 0.8 copy-start.3
